TPU v7x, 32 devices: a whole 2x2x4 slice. The times are simulated.
32 devices in a mesh: req: 8 (over z, y), mp: 4 (over x, core).
Axes of the slice: x: 2, y: 2, z: 4, core: 2. Of those that a mesh axis runs over, the one named last changes fastest.
Arguments:
- cand_feats: bfloat16 [4096, 1024], P('req', 'mp'), may hold values from -6 to 6
- cand_perm: int32 [8, 512], P('req'), may hold values from 0 to 511, each once within a row
- w_in: bfloat16 [1024, 4, 1024], P(None, None, 'mp'), may hold values from -0.1875 to 0.1875
- w_out: bfloat16 [1024, 1024], P('mp'), may hold values from -0.1875 to 0.1875
- cache_k: bfloat16 [256, 32, 1024], P('req', None, 'mp'), may hold values from -6 to 6
- cache_v: bfloat16 [256, 32, 1024], P('req', None, 'mp'), may hold values from -1.5 to 1.5
- hist_len: int32 [8], P('req'), may hold values from 1 to 4096, as said below
- hist_home: int32 [8], replicated, may hold values from 0 to 7
- hist_slot: int32 [8, 128], replicated, may hold values from 0 to 31
- hist_mask: int32 [8, 4, 128], P('req'), may hold values 0 or 1
Outputs:
- scored: bfloat16 [4096, 1024], P('req', 'mp')
Inputs may be any that keep to these rules, and one draw needn't show every extreme that they name: `cand_perm`: each row is a permutation of 0 to 511. `hist_len`: some request has a history of 4096 events.
All inputs are finite; a program needn't handle non-finite values. No bound on the sum of `hist_mask` on one device may be relied on, other than what follows from the above.
Results may differ from a plain program's by a relative error of at most 0.0067.
Values may be sent and summed in bfloat16 or wider, within the bound.
A program may use at most 64 MiB of HBM per device.

v0:
```python
import jax
import jax.numpy as jnp
from jax import lax
from jax.sharding import PartitionSpec as P

HEADS = 8
DH = 128
BLK = 32
MAXBLK = 128
GROUP = 128


EPS = 1e-05


def local(
    cand_feats, cand_perm, w_in, w_out, cache_k, cache_v, hist_len, hist_home, hist_slot, hist_mask
):
    shards = lax.axis_size("req")
    own_index = lax.axis_index("req")
    columns = cand_feats.shape[1]
    cand_slot = cand_feats.shape[0] // shards
    arrived = lax.all_to_all(
        cand_feats.reshape(shards, cand_slot, columns),
        "req",
        split_axis=0,
        concat_axis=0,
        tiled=True,
    )
    arrived = arrived.reshape(shards * cand_slot, columns)
    own_rows = jnp.take(arrived, cand_perm[0], axis=0)
    full_rows = lax.all_gather(own_rows, "mp", axis=1, tiled=True)
    cand_count = full_rows.shape[0]
    features = full_rows.astype(jnp.float32)
    centred = features - jnp.mean(features, axis=1, keepdims=True)
    spread = jnp.mean(centred * centred, axis=1, keepdims=True)
    normed = (centred * lax.rsqrt(spread + EPS)).astype(jnp.bfloat16)
    local_width = w_in.shape[2]
    parts = jax.nn.silu(
        jnp.dot(
            normed, w_in.reshape(w_in.shape[0], 4 * local_width), preferred_element_type=jnp.float32
        )
    ).astype(jnp.bfloat16)
    parts = parts.reshape(cand_count, 4, local_width)
    gate_u, value_v, query_q, key_k = (parts[:, 0], parts[:, 1], parts[:, 2], parts[:, 3])
    rounds_here = MAXBLK // shards
    offsets = (own_index - hist_home) % shards
    wanted = offsets[:, None] + jnp.arange(rounds_here, dtype=jnp.int32)[None, :] * shards
    slots = jnp.take_along_axis(hist_slot, wanted, axis=1)
    send_keys = jnp.take(cache_k, slots, axis=0)
    send_values = jnp.take(cache_v, slots, axis=0)
    key_count = MAXBLK * BLK
    own_len = hist_len[0]
    got_keys, got_values = (
        lax.all_to_all(send_keys, "req", split_axis=0, concat_axis=0, tiled=True),
        lax.all_to_all(send_values, "req", split_axis=0, concat_axis=0, tiled=True),
    )
    live_keys = (jnp.arange(key_count, dtype=jnp.int32) < own_len).astype(jnp.float32)
    home_block = hist_home[own_index]
    block_order = jnp.arange(MAXBLK, dtype=jnp.int32)
    source = (home_block + block_order % shards) % shards
    round_at = block_order // shards
    hist_keys = got_keys[source, round_at].reshape(key_count, local_width)
    hist_values = got_values[source, round_at].reshape(key_count, local_width)
    block_mask = jnp.repeat(hist_mask[0].astype(jnp.float32), BLK, axis=1) * live_keys[None, :]
    score_scale = DH ** (-0.5)
    outputs = []
    for head_index in range(local_width // DH):
        lo_col = head_index * DH
        q_head = query_q[:, lo_col : lo_col + DH]
        scores = (
            lax.dot_general(
                q_head,
                hist_keys[:, lo_col : lo_col + DH],
                (((1,), (1,)), ((), ())),
                preferred_element_type=jnp.float32,
            )
            * score_scale
        )
        weights = (
            jax.nn.silu(scores).reshape(cand_count // GROUP, GROUP, key_count)
            * block_mask[:, None, :]
        )
        weights = weights.reshape(cand_count, key_count).astype(jnp.bfloat16)
        own_score = (
            jnp.sum(
                q_head.astype(jnp.float32) * key_k[:, lo_col : lo_col + DH].astype(jnp.float32),
                axis=1,
                keepdims=True,
            )
            * score_scale
        )
        own_term = jax.nn.silu(own_score) * value_v[:, lo_col : lo_col + DH].astype(jnp.float32)
        outputs.append(
            jnp.dot(
                weights, hist_values[:, lo_col : lo_col + DH], preferred_element_type=jnp.float32
            )
            + own_term
        )
    attn = jnp.concatenate(outputs, axis=1)
    width_all = HEADS * DH
    row_total = lax.psum(jnp.sum(attn, axis=1, keepdims=True), "mp")
    attn_mean = row_total / width_all
    attn_centred = attn - attn_mean
    square_total = lax.psum(jnp.sum(attn_centred * attn_centred, axis=1, keepdims=True), "mp")
    attn_spread = square_total / width_all
    hidden = (attn_centred * lax.rsqrt(attn_spread + EPS) * gate_u.astype(jnp.float32)).astype(
        jnp.bfloat16
    )
    mixed = lax.psum_scatter(
        lax.dot_general(
            w_out, hidden, (((0,), (1,)), ((), ())), preferred_element_type=jnp.float32
        ),
        "mp",
        scatter_dimension=0,
        tiled=True,
    ).T
    return (own_rows.astype(jnp.float32) + mixed).astype(jnp.bfloat16)


def solution(mesh):
    in_specs = (
        P("req", "mp"),
        P("req", None),
        P(None, None, "mp"),
        P("mp", None),
        P("req", None, "mp"),
        P("req", None, "mp"),
        P("req"),
        P(),
        P(),
        P("req", None, None),
    )
    out_specs = P("req", "mp")
    return jax.shard_map(local, mesh=mesh, in_specs=in_specs, out_specs=out_specs, check_vma=False)
```

profile of v0, /device:TPU:1, one launch (start us, length us, event | category | flops | bytes accessed | tf_op | source)
XLA Modules:
  0.0 192.9 jit_solution(16524233919808506970)
XLA Ops:
  6.5 6.5 %all-to-all-start = ((bf16[8,64,256]{2,1,0:T(8,128)(2,1)}), bf16[8,64,256]{2,1,0:T(8,128)(2,1)S(1)}, u32[]{:S(2)}, u32[]{:S(2)}) async-start(bf16[8,64,256]{2,1,0:T(8,128)(2,1)} %bitcast.70), calls=%async_computation | async-start | bytes 524288 | tf_op jit(solution)/shard_map/all_to_all | solution.py:23
  16.2 2.0 %gather_fusion.4 = bf16[128,32,256]{2,1,0:T(8,128)(2,1)} fusion(bf16[32,32,256]{2,1,0:T(8,128)(2,1)S(1)} %copy-done.3, s32[1024]{0:T(1024)S(1)} %pad_clamp_fusion), kind=kCustom, calls=%fused_computation.clone | custom fusion | bytes 4194816 | tf_op jit(solution)/shard_map/jit(_take)/gather | solution.py:50
  18.2 4.0 %broadcast_select_fusion = (bf16[8,16,32,256]{3,2,1,0:T(8,128)(2,1)}, bf16[8,16,32,256]{3,2,1,0:T(8,128)(2,1)}) fusion(bf16[8,16,32,256]{3,2,1,0:T(8,128)(2,1)S(1)} %bitcast.56, pred[8,16]{1,0:T(8,128)(4,1)S(1)} %get-tuple-element.8, bf16[8,16,32,256]{3,2,1,0:T(8,128)(2,1)} %bitcast.57), kind=kLoop, calls=%fused_computation.17 | loop fusion | flops 2097152 | bytes 8388736 | tf_op jit(solution)/shard_map/jit(_take)/select_n | solution.py:51
  22.2 5.6 %all-to-all-start.1 = ((bf16[8,16,32,256]{3,2,1,0:T(8,128)(2,1)}), bf16[8,16,32,256]{3,2,1,0:T(8,128)(2,1)S(1)}, u32[]{:S(2)}, u32[]{:S(2)}) async-start(bf16[8,16,32,256]{3,2,1,0:T(8,128)(2,1)} %get-tuple-element.15), calls=%async_computation.1 | async-start | bytes 4194304 | tf_op jit(solution)/shard_map/all_to_all | solution.py:55
  27.8 2.0 %gather_fusion = bf16[512,256]{1,0:T(8,128)(2,1)S(1)} fusion(bf16[512,256]{1,0:T(8,128)(2,1)S(1)} %bitcast.55, s32[1024]{0:T(1024)S(1)} %pad_clamp_fusion.1), kind=kCustom, calls=%fused_computation.2 | custom fusion | bytes 526336 | tf_op jit(solution)/shard_map/jit(_take)/gather | solution.py:31
  30.7 43.9 %all-to-all-done.1 = bf16[8,16,32,256]{3,2,1,0:T(8,128)(2,1)S(1)} async-done(((bf16[8,16,32,256]{3,2,1,0:T(8,128)(2,1)}), bf16[8,16,32,256]{3,2,1,0:T(8,128)(2,1)S(1)}, u32[]{:S(2)}, u32[]{:S(2)}) %all-to-all-start.1) | async-done | bytes 2097184 | tf_op jit(solution)/shard_map/all_to_all | solution.py:55
  75.9 5.3 %all-to-all-start.2 = ((bf16[8,16,32,256]{3,2,1,0:T(8,128)(2,1)}), bf16[8,16,32,256]{3,2,1,0:T(8,128)(2,1)}, u32[]{:S(2)}, u32[]{:S(2)}) async-start(bf16[8,16,32,256]{3,2,1,0:T(8,128)(2,1)} %get-tuple-element.14), calls=%async_computation.2 | async-start | bytes 4194304 | tf_op jit(solution)/shard_map/all_to_all | solution.py:56
  82.9 2.1 %copy.22 = bf16[128,8,4,256]{3,1,2,0:T(8,128)(2,1)S(1)} copy(bf16[128,8,4,256]{3,2,1,0:T(4,128)(2,1)} %bitcast.65) | data formatting | bytes 4194304
  88.9 2.6 %multiply_convert_fusion = bf16[512,1024]{1,0:T(8,128)(2,1)} fusion(bf16[1024,1024]{1,0:T(8,128)(2,1)S(1)} %bitcast.66, bf16[512,1024]{1,0:T(8,128)(2,1)S(1)} %copy-done.7, f32[512]{0:T(512)S(1)} %add_rsqrt_fusion.1, f32[512]{0:T(512)S(1)} %broadcast_multiply_fusion.2), kind=kOutput, calls=%fused_computation.16 | convolution fusion | flops 1078460416 | bytes 4198400 | tf_op jit(solution)/shard_map/dot_general | solution.py:40
  91.5 1.9 reshape.327
  93.3 2.5 %fusion.41 = (bf16[512,1,256]{2,1,0:T(2,128)(2,1)}, bf16[512,1,256]{2,1,0:T(2,128)(2,1)S(1)}, bf16[512,1,256]{2,1,0:T(2,128)(2,1)}, bf16[512,1,256]{2,1,0:T(2,128)(2,1)}) fusion(bf16[512,4,256]{2,1,0:T(4,128)(2,1)S(1)} %reshape.327), kind=kLoop, calls=%fused_computation.93 | loop fusion | bytes 2097152 | tf_op jit(solution)/shard_map/slice | solution.py:45
  95.8 2.0 %copy.21 = bf16[512,1,256]{0,2,1:T(8,128)(2,1)} copy(bf16[512,1,256]{2,1,0:T(2,128)(2,1)} %get-tuple-element.10) | data formatting | bytes 524288
  102.3 2.2 %gather_fusion.1 = bf16[128,32,256]{2,1,0:T(8,128)(2,1)} fusion(bf16[8,16,32,256]{3,2,1,0:T(8,128)(2,1)S(1)} %copy-done.5, s32[128]{0:T(128)S(1)} %fusion.39), kind=kCustom, calls=%fused_computation.3 | custom fusion | bytes 4195328 | tf_op jit(solution)/shard_map/gather | solution.py:63
  104.4 5.7 %fusion.1 = bf16[512,4096]{1,0:T(8,128)(2,1)} fusion(f32[4,4096]{1,0:T(4,128)S(1)} %broadcast_multiply_fusion, bf16[4096,256]{1,0:T(8,128)(2,1)} %bitcast.60, bf16[512,256]{1,0:T(8,128)(2,1)S(1)} %bitcast.63), kind=kOutput, calls=%fused_computation.9 | convolution fusion | flops 551550976 | bytes 5439488 | tf_op jit(solution)/shard_map/dot_general | solution.py:72
  110.2 4.3 %fusion = bf16[512,4096]{1,0:T(8,128)(2,1)} fusion(f32[4,4096]{1,0:T(4,128)S(1)} %broadcast_multiply_fusion, bf16[4096,256]{1,0:T(8,128)(2,1)S(1)} %bitcast.61, bf16[512,256]{1,0:T(8,128)(2,1)S(1)} %bitcast.64), kind=kOutput, calls=%fused_computation.8 | convolution fusion | flops 551550976 | bytes 5439488 | tf_op jit(solution)/shard_map/dot_general | solution.py:72
  114.5 13.7 %all-to-all-done.2 = bf16[8,16,32,256]{3,2,1,0:T(8,128)(2,1)} async-done(((bf16[8,16,32,256]{3,2,1,0:T(8,128)(2,1)}), bf16[8,16,32,256]{3,2,1,0:T(8,128)(2,1)}, u32[]{:S(2)}, u32[]{:S(2)}) %all-to-all-start.2) | async-done | bytes 2097184 | tf_op jit(solution)/shard_map/all_to_all | solution.py:56
  128.2 2.5 %gather_fusion.2 = bf16[128,32,256]{2,1,0:T(8,128)(2,1)S(1)} fusion(bf16[8,16,32,256]{3,2,1,0:T(8,128)(2,1)} %all-to-all-done.2, s32[128]{0:T(128)S(1)} %fusion.39), kind=kCustom, calls=%fused_computation.4 | custom fusion | bytes 4195328 | tf_op jit(solution)/shard_map/gather | solution.py:64
  130.7 3.9 %fusion.43 = (f32[512]{0:T(512)S(1)}, f32[512,128]{0,1:T(8,128)S(1)}) fusion(bf16[512,256]{0,1:T(8,128)(2,1)S(1)} %bitcast.67, f32[512]{0:T(512)S(1)} %get-tuple-element.20, bf16[512,4096]{1,0:T(8,128)(2,1)} %fusion.1, bf16[4096,256]{1,0:T(8,128)(2,1)S(1)} %bitcast.58), kind=kOutput, calls=%fused_computation.95 | convolution fusion | flops 537132544 | bytes 5640192 | tf_op jit(solution)/shard_map/dot_general | solution.py:95
  134.6 2.4 %fusion.42 = (f32[512]{0:T(512)S(1)}, f32[512,128]{0,1:T(8,128)S(1)}) fusion(bf16[512,256]{0,1:T(8,128)(2,1)} %bitcast.68, f32[512]{0:T(512)S(1)} %get-tuple-element.21, bf16[512,4096]{1,0:T(8,128)(2,1)S(1)} %copy-done.2, bf16[4096,256]{1,0:T(8,128)(2,1)S(1)} %bitcast.59), kind=kOutput, calls=%fused_computation.94 | convolution fusion | flops 537132544 | bytes 5640192 | tf_op jit(solution)/shard_map/dot_general | solution.py:95
  137.0 7.3 %psum.14 = f32[512,1]{0,1:T(1,128)S(1)} all-reduce(f32[512,1]{0,1:T(1,128)S(1)} %bitcast.74), channel_id=1, replica_groups=mesh['req'=8,'mp'=4] {'mp'}, use_global_device_ids=true, to_apply=%region_6.8 | all-reduce | flops 512 | bytes 4096 | tf_op jit(solution)/shard_map/psum | solution.py:102
  144.4 5.8 %psum.15 = f32[512,1]{0,1:T(1,128)S(1)} all-reduce(f32[512,1]{0,1:T(1,128)S(1)} %bitcast.73), channel_id=1, replica_groups=mesh['req'=8,'mp'=4] {'mp'}, use_global_device_ids=true, to_apply=%region_8.10 | all-reduce | flops 512 | bytes 4096 | tf_op jit(solution)/shard_map/psum | solution.py:105
  150.2 3.0 %convolution_bitcast_fusion = f32[1024,512]{0,1:T(8,128)} fusion(bf16[256,1024]{1,0:T(8,128)(2,1)} %param.15, f32[512,128]{0,1:T(8,128)S(1)} %get-tuple-element.19, f32[512,128]{0,1:T(8,128)S(1)} %get-tuple-element.17, bf16[512,1,256]{0,2,1:T(8,128)(2,1)} %copy.21, f32[512]{0:T(512)S(1)} %bitcast.77, f32[512]{0:T(512)S(1)} %bitcast.72), kind=kOutput, calls=%fused_computation.19 | convolution fusion | flops 269221888 | bytes 3411968 | tf_op jit(solution)/shard_map/dot_general | solution.py:111
  153.2 31.0 %reduce-scatter.2.cloned.1.call-done = f32[256,512]{0,1:T(8,128)} async-done(((f32[1024,512]{0,1:T(8,128)}), f32[256,512]{0,1:T(8,128)}) %reduce-scatter.2.cloned.1.call-update) | async-done | bytes 524304 | tf_op jit(solution)/shard_map/reduce_scatter | solution.py:110
  184.2 1.9 fusion.17
  (64 shorter events, 14.8 us)
Async XLA Ops:
  6.5 8.6 %copy-start = (bf16[32,32,256]{2,1,0:T(8,128)(2,1)S(1)}, bf16[32,32,256]{2,1,0:T(8,128)(2,1)}, u32[]{:S(2)}) copy-start(bf16[32,32,256]{2,1,0:T(8,128)(2,1)} %param.17) | copy-start | bytes 1572868
  6.5 7.4 %copy-start.1 = (s32[8,128]{1,0:T(8,128)S(1)}, s32[8,128]{1,0:T(8,128)}, u32[]{:S(2)}) copy-start(s32[8,128]{1,0:T(8,128)} %param.20) | copy-start | bytes 12292
  6.5 15.6 %all-to-all-start = ((bf16[8,64,256]{2,1,0:T(8,128)(2,1)}), bf16[8,64,256]{2,1,0:T(8,128)(2,1)S(1)}, u32[]{:S(2)}, u32[]{:S(2)}) async-start(bf16[8,64,256]{2,1,0:T(8,128)(2,1)} %bitcast.70), calls=%async_computation | async-start | bytes 524288 | tf_op jit(solution)/shard_map/all_to_all | solution.py:23
  15.1 1.0 copy-start.3
  22.2 5.6 %copy-start.9 = (s32[1,512]{1,0:T(1,128)S(1)}, s32[1,512]{1,0:T(1,128)}, u32[]{:S(2)}) copy-start(s32[1,512]{1,0:T(1,128)} %param.13) | copy-start | bytes 6148
  22.2 52.4 %all-to-all-start.1 = ((bf16[8,16,32,256]{3,2,1,0:T(8,128)(2,1)}), bf16[8,16,32,256]{3,2,1,0:T(8,128)(2,1)S(1)}, u32[]{:S(2)}, u32[]{:S(2)}) async-start(bf16[8,16,32,256]{3,2,1,0:T(8,128)(2,1)} %get-tuple-element.15), calls=%async_computation.1 | async-start | bytes 4194304 | tf_op jit(solution)/shard_map/all_to_all | solution.py:55
  27.7 57.9 %all-gather.2.cloned.1.call-start = ((), (), s32[]{:S(2)}) async-start(), calls=%async_computation.4 | async-start | bytes 1310720 | tf_op jit(solution)/shard_map/all_gather | solution.py:32
  74.5 1.3 copy-start.4
  74.5 7.5 %copy-start.11 = (s32[8]{0:T(128)S(1)}, s32[8]{0:T(128)}, u32[]{:S(2)}) copy-start(s32[8]{0:T(128)} %param.19) | copy-start | bytes 100
  74.5 8.1 %copy-start.10 = (s32[1,4,128]{2,1,0:T(4,128)S(1)}, s32[1,4,128]{2,1,0:T(4,128)}, u32[]{:S(2)}) copy-start(s32[1,4,128]{2,1,0:T(4,128)} %param.21) | copy-start | bytes 6148
  75.9 52.3 %all-to-all-start.2 = ((bf16[8,16,32,256]{3,2,1,0:T(8,128)(2,1)}), bf16[8,16,32,256]{3,2,1,0:T(8,128)(2,1)}, u32[]{:S(2)}, u32[]{:S(2)}) async-start(bf16[8,16,32,256]{3,2,1,0:T(8,128)(2,1)} %get-tuple-element.14), calls=%async_computation.2 | async-start | bytes 4194304 | tf_op jit(solution)/shard_map/all_to_all | solution.py:56
  81.1 103.0 %reduce-scatter.2.cloned.1.call-start = ((), (), s32[]{:S(2)}) async-start(), calls=%async_computation.5 | async-start | bytes 2621440 | tf_op jit(solution)/shard_map/reduce_scatter | solution.py:110
  85.7 3.2 %copy-start.7 = (bf16[512,1024]{1,0:T(8,128)(2,1)S(1)}, bf16[512,1024]{1,0:T(8,128)(2,1)}, u32[]{:S(2)}) copy-start(bf16[512,1024]{1,0:T(8,128)(2,1)} %all-gather.2.cloned.1.call-done) | copy-start | bytes 3145732
  95.8 6.4 %copy-start.5 = (bf16[8,16,32,256]{3,2,1,0:T(8,128)(2,1)S(1)}, bf16[8,16,32,256]{3,2,1,0:T(8,128)(2,1)}, u32[]{:S(2)}) copy-start(bf16[8,16,32,256]{3,2,1,0:T(8,128)(2,1)} %copy-done.4) | copy-start | bytes 6291460
  100.9 29.7 %copy-start.8 = (bf16[512,1,256]{0,2,1:T(8,128)(2,1)}, bf16[512,1,256]{0,2,1:T(8,128)(2,1)S(1)}, u32[]{:S(2)}) copy-start(bf16[512,1,256]{0,2,1:T(8,128)(2,1)S(1)} %copy.20) | copy-start | bytes 786436
  104.4 5.7 %copy-start.6 = (bf16[128,32,256]{2,1,0:T(8,128)(2,1)S(1)}, bf16[128,32,256]{2,1,0:T(8,128)(2,1)}, u32[]{:S(2)}) copy-start(bf16[128,32,256]{2,1,0:T(8,128)(2,1)} %gather_fusion.1) | copy-start | bytes 6291460
  130.6 3.9 %copy-start.2 = (bf16[512,4096]{1,0:T(8,128)(2,1)S(1)}, bf16[512,4096]{1,0:T(8,128)(2,1)}, u32[]{:S(2)}) copy-start(bf16[512,4096]{1,0:T(8,128)(2,1)} %fusion) | copy-start | bytes 12582916
Sparse Core Ops, SparseCore 0:
  30.8 19.4 all-gather.1
  153.3 30.8 reduce-scatter.1
where the time goes:
time: 194 us; the launch traced here: 193 us
  waiting for transfers between devices  88.6 us (46%)
  local copies, waits for them, and re-layouts  24.6 us (13%)
  matrix products  21.9 us (11%)
  starting transfers between devices  17.6 us (9%)
  between operations  14.3 us (7%)
  blocking collectives  13.1 us (7%)
  other arithmetic  12.8 us (7%)
    all_to_all x1, waiting for transfers between devices, local(): lax.all_to_all(send_keys, 'req', split_axis=0, concat_axis=0, tiled=True)  43.9 us
    reduce_scatter x1, waiting for transfers between devices, local(): lax.psum_scatter(lax.dot_general(w_out, hidden, (((0,), (1,)), ((), ())),...  31 us
    all_to_all x1, waiting for transfers between devices, local(): lax.all_to_all(send_values, 'req', split_axis=0, concat_axis=0, tiled=True)  13.7 us
    dot_general x2, matrix products, local(): lax.dot_general(q_head, hist_keys[:, lo_col:lo_col + DH], (((1,), (1,)),...  10 us
    unnamed x29, local copies, waits for them, and re-layouts  8.9 us
    psum x1, blocking collectives, local(): row_total = lax.psum(jnp.sum(attn, axis=1, keepdims=True), 'mp')  7.3 us
    all_to_all x1, starting transfers between devices, local(): lax.all_to_all(cand_feats.reshape(shards, cand_slot, columns), 'req', spl...  6.51 us
    dot_general x2, matrix products, local(): jnp.dot(weights, hist_values[:, lo_col:lo_col + DH], preferred_element_ty...  6.33 us
  transfers between devices with their start and end apart: 5, of which 3 were waited for; matrix products, arithmetic and copies ran while one was open for 23% of the time, Pallas kernels for 0%

commit v1 on v0

--- a/solution.py
+++ b/solution.py
@@ -1,6 +1,10 @@
+import functools
+
 import jax
 import jax.numpy as jnp
 from jax import lax
+from jax.experimental import pallas as pl
+from jax.experimental.pallas import tpu as pltpu
 from jax.sharding import PartitionSpec as P
 
 HEADS = 8
@@ -13,7 +17,7 @@
 EPS = 1e-05
 
 
-def local(
+def move_blocks(
     cand_feats, cand_perm, w_in, w_out, cache_k, cache_v, hist_len, hist_home, hist_slot, hist_mask
 ):
     shards = lax.axis_size("req")
@@ -118,6 +122,485 @@
     return (own_rows.astype(jnp.float32) + mixed).astype(jnp.bfloat16)
 
 
+def remote(src, dst, send_sem, recv_sem, device):
+    return pltpu.make_async_remote_copy(
+        src_ref=src,
+        dst_ref=dst,
+        send_sem=send_sem,
+        recv_sem=recv_sem,
+        device_id=device,
+        device_id_type=pl.DeviceIdType.MESH,
+    )
+
+
+def half_silu(half):
+    return half + half * jnp.tanh(half)
+
+
+def kernel(
+    shards,
+    feats,
+    perm,
+    w_in,
+    w_out,
+    cache_k,
+    cache_v,
+    counts,
+    home,
+    slot,
+    out,
+    rows_all,
+    normed,
+    own_rows,
+    q_all,
+    u_all,
+    v_own,
+    k_own,
+    wo_all,
+    other_k,
+    other_v,
+    counts_all,
+    hist_k,
+    hist_v,
+    mask,
+    part_out,
+    part_in,
+    total,
+    attn_all,
+    row_s,
+    row_r,
+    core_s,
+    core_r,
+    x_s,
+    x_r,
+    fwd_s,
+    fwd_r,
+    kv_s,
+    kv_r,
+    cnt_s,
+    cnt_r,
+    wo_s,
+    wo_r,
+    q_s,
+    q_r,
+    p_s,
+    p_r,
+    u_s,
+    u_r,
+    a_s,
+    a_r,
+):
+    me = lax.axis_index("req")
+    mp = lax.axis_index("mp")
+    lines = shards // 2
+    line, side = me // 2, me % 2
+    mate = line * 2 + (1 - side)
+    core_mp = (mp // 2) * 2 + (1 - mp % 2)
+    x_mp = (1 - mp // 2) * 2 + mp % 2
+    far_mp = (1 - mp // 2) * 2 + (1 - mp % 2)
+    slots = feats.shape[1]
+    width = feats.shape[2]
+    cands = shards * slots
+    groups = cands // GROUP
+    rounds = MAXBLK // shards
+    keys_here = rounds * BLK
+    core, across, side_mate = (me, core_mp), (me, x_mp), (mate, mp)
+
+    barrier = pltpu.get_barrier_semaphore()
+    for step in range(1, shards):
+        pl.semaphore_signal(
+            barrier, inc=1, device_id=((me + step) % shards, mp), device_id_type=pl.DeviceIdType.MESH
+        )
+    for step in range(1, 4):
+        pl.semaphore_signal(
+            barrier, inc=1, device_id=(me, (mp + step) % 4), device_id_type=pl.DeviceIdType.MESH
+        )
+    pl.semaphore_wait(barrier, shards + 2)
+
+    def row_copy(source, target):
+        return remote(
+            feats.at[target],
+            rows_all.at[mp, pl.ds(source * slots, slots)],
+            row_s.at[target],
+            row_r.at[source],
+            (target, mp),
+        )
+
+    def count_copy(source, target):
+        return remote(
+            counts, counts_all.at[source], cnt_s.at[target], cnt_r.at[source], (target * 2 + side, mp)
+        )
+
+    def out_weight_copy(source, target):
+        return remote(
+            w_out.at[:, pl.ds(pl.multiple_of(target * width, width), width)],
+            wo_all.at[source],
+            wo_s.at[target],
+            wo_r.at[source],
+            (me, target),
+        )
+
+    def chunk(part, source):
+        return rows_all.at[part, pl.ds(source * slots, slots)]
+
+    def core_copy(source):
+        return remote(chunk(mp, source), chunk(mp, source), core_s.at[source], core_r.at[source], core)
+
+    def x_copy(source):
+        return remote(chunk(mp, source), chunk(mp, source), x_s.at[source], x_r.at[source], across)
+
+    def fwd_copy(source):
+        return remote(chunk(x_mp, source), chunk(x_mp, source), fwd_s.at[source], fwd_r.at[source], core)
+
+    def core_got(source):
+        return remote(
+            chunk(core_mp, source), chunk(core_mp, source), core_s.at[source], core_r.at[source], core
+        )
+
+    def x_got(source):
+        return remote(chunk(x_mp, source), chunk(x_mp, source), x_s.at[source], x_r.at[source], across)
+
+    def fwd_got(source):
+        return remote(
+            chunk(far_mp, source), chunk(far_mp, source), fwd_s.at[source], fwd_r.at[source], core
+        )
+
+    keys_copy = remote(cache_k, other_k, kv_s.at[0], kv_r.at[0], side_mate)
+    values_copy = remote(cache_v, other_v, kv_s.at[1], kv_r.at[1], side_mate)
+
+    @pl.loop(1, shards)
+    def _(step):
+        row_copy(me, (me + step) % shards).start()
+
+    for step in range(1, lines):
+        count_copy(line, (line + step) % lines).start()
+    keys_copy.start()
+    values_copy.start()
+    rows_all[mp, pl.ds(me * slots, slots), :] = feats[me]
+    counts_all[line] = counts[...]
+    core_copy(me).start()
+    x_copy(me).start()
+
+    @pl.loop(1, shards)
+    def _(step):
+        source = (me + step) % shards
+        row_copy(source, me).wait_recv()
+        core_copy(source).start()
+        x_copy(source).start()
+
+    for step in range(1, 4):
+        out_weight_copy(mp, (mp + step) % 4).start()
+    wo_all[mp] = w_out[:, pl.ds(pl.multiple_of(mp * width, width), width)]
+
+    def gather(keys_ref, values_ref, shard, half):
+        @pl.loop(0, lines)
+        def _(at):
+            request = at * 2 + side
+            first = lax.rem(shard - home[request] + shards, shards)
+
+            @pl.loop(0, rounds)
+            def _(turn):
+                place = slot[request, first + turn * shards]
+                rows = pl.ds(half * keys_here + turn * BLK, BLK)
+                hist_k[at, rows, :] = keys_ref[place]
+                hist_v[at, rows, :] = values_ref[place]
+
+    gather(cache_k, cache_v, me, 0)
+
+    @pl.loop(0, shards)
+    def _(step):
+        source = (me + step) % shards
+        x_got(source).wait_recv()
+        fwd_copy(source).start()
+
+    for step in range(1, lines):
+        count_copy((line + step) % lines, line).wait_recv()
+
+    @pl.loop(0, lines)
+    def _(at):
+        request = at * 2 + side
+        number = counts_all[at].astype(jnp.bfloat16)
+        for half, shard in enumerate((me, mate)):
+            first = lax.rem(shard - home[request] + shards, shards)
+            key_at = lax.broadcasted_iota(jnp.int32, (MAXBLK, keys_here), 1)
+            block_at = lax.broadcasted_iota(jnp.int32, (MAXBLK, keys_here), 0)
+            spread = (block_at == first + (key_at // BLK) * shards).astype(jnp.float32)
+            live = jnp.dot(number, spread.astype(jnp.bfloat16), preferred_element_type=jnp.float32)
+            place = lax.broadcasted_iota(jnp.int32, live.shape, 1) % BLK
+            mask[at, :, half * keys_here : (half + 1) * keys_here] = jnp.where(
+                place.astype(jnp.float32) < live, 0.5 * DH ** (-0.5), 0.0
+            )
+
+    @pl.loop(0, shards)
+    def _(step):
+        source = (me + step) % shards
+        core_got(source).wait_recv()
+        fwd_got(source).wait_recv()
+
+    def q_copy(source, target, group):
+        rows = pl.ds(group * GROUP, GROUP)
+        return remote(
+            q_all.at[source, rows],
+            q_all.at[source, rows],
+            q_s.at[target * groups + group],
+            q_r.at[source * groups + group],
+            (target * 2 + side, mp),
+        )
+
+    def project(part, group):
+        rows = pl.ds(group * GROUP, GROUP)
+        scores = jnp.dot(normed[rows, :], w_in[part], preferred_element_type=jnp.float32)
+        return half_silu(0.5 * scores).astype(jnp.bfloat16)
+
+    @pl.loop(0, groups)
+    def _(group):
+        rows = pl.ds(group * GROUP, GROUP)
+        wanted = perm[rows, :]
+        pick = (lax.broadcasted_iota(jnp.int32, (GROUP, cands), 1) == wanted).astype(jnp.float32)
+        pick = pick.astype(jnp.bfloat16)
+        features = jnp.concatenate(
+            [jnp.dot(pick, rows_all[part], preferred_element_type=jnp.float32) for part in range(4)],
+            axis=1,
+        )
+        own_rows[rows, :] = jnp.dot(pick, rows_all[mp], preferred_element_type=jnp.float32)
+        centred = features - jnp.mean(features, axis=1, keepdims=True)
+        variance = jnp.mean(centred * centred, axis=1, keepdims=True)
+        normed[rows, :] = (centred * lax.rsqrt(variance + EPS)).astype(jnp.bfloat16)
+        q_all[line, rows, :] = project(2, group)
+        for step in range(1, lines):
+            q_copy(line, (line + step) % lines, group).start()
+
+    @pl.loop(0, groups)
+    def _(group):
+        u_all[mp, pl.ds(group * GROUP, GROUP), :] = project(0, group)
+
+    def part_copy(buffer, part, sems, index, device):
+        send, receive = sems
+        return remote(buffer.at[part], buffer.at[part], send.at[index], receive.at[index], device)
+
+    u_sems = (u_s, u_r)
+    part_copy(u_all, mp, u_sems, 0, core).start()
+    part_copy(u_all, mp, u_sems, 1, across).start()
+
+    @pl.loop(0, groups)
+    def _(group):
+        rows = pl.ds(group * GROUP, GROUP)
+        v_own[rows, :] = project(1, group)
+        k_own[rows, :] = project(3, group)
+
+    keys_copy.wait_recv()
+    values_copy.wait_recv()
+    gather(other_k, other_v, mate, 1)
+
+    def attend(at, group):
+        rows = pl.ds(group * GROUP, GROUP)
+        scale = mask[at, pl.ds(group, 1), :]
+        heads = []
+        for lo in range(0, width, DH):
+            query = q_all[at, rows, lo : lo + DH]
+            summed = None
+            for first in range(0, 2 * keys_here, keys_here):
+                scores = lax.dot_general(
+                    query,
+                    hist_k[at, first : first + keys_here, lo : lo + DH],
+                    (((1,), (1,)), ((), ())),
+                    preferred_element_type=jnp.float32,
+                )
+                weights = half_silu(scores * scale[:, first : first + keys_here]).astype(jnp.bfloat16)
+                term = jnp.dot(
+                    weights,
+                    hist_v[at, first : first + keys_here, lo : lo + DH],
+                    preferred_element_type=jnp.float32,
+                )
+                summed = term if summed is None else summed + term
+            heads.append(summed)
+        return jnp.concatenate(heads, axis=1)
+
+    def p_copy(source, target, group):
+        rows = pl.ds(group * GROUP, GROUP)
+        return remote(
+            part_out.at[target, rows],
+            part_in.at[source, rows],
+            p_s.at[target * groups + group],
+            p_r.at[source * groups + group],
+            (target * 2 + side, mp),
+        )
+
+    @pl.loop(0, groups)
+    def _(group):
+        for step in range(1, lines):
+            at = (line + step) % lines
+            q_copy(at, line, group).wait_recv()
+            part_out[at, pl.ds(group * GROUP, GROUP), :] = attend(at, group).astype(jnp.bfloat16)
+            p_copy(line, at, group).start()
+
+    part_copy(u_all, x_mp, u_sems, 1, across).wait_recv()
+    part_copy(u_all, x_mp, u_sems, 2, core).start()
+
+    @pl.loop(0, groups)
+    def _(group):
+        rows = pl.ds(group * GROUP, GROUP)
+        own = []
+        for lo in range(0, width, DH):
+            query = q_all[line, rows, lo : lo + DH].astype(jnp.float32)
+            key = k_own[rows, lo : lo + DH].astype(jnp.float32)
+            half = jnp.sum(query * key, axis=1, keepdims=True) * (0.5 * DH ** (-0.5))
+            own.append(half_silu(half) * v_own[rows, lo : lo + DH].astype(jnp.float32))
+        total[rows, :] = attend(line, group) + jnp.concatenate(own, axis=1)
+
+    part_copy(u_all, core_mp, u_sems, 0, core).wait_recv()
+    part_copy(u_all, far_mp, u_sems, 2, core).wait_recv()
+    for step in range(1, 4):
+        out_weight_copy((mp + step) % 4, mp).wait_recv()
+
+    def attn_copy(part, kind, group, device):
+        piece = attn_all.at[part, pl.ds(group * GROUP, GROUP)]
+        index = kind * groups + group
+        return remote(piece, piece, a_s.at[index], a_r.at[index], device)
+
+    def collect(group):
+        rows = pl.ds(group * GROUP, GROUP)
+        summed = total[rows, :]
+        for step in range(1, lines):
+            at = (line + step) % lines
+            p_copy(at, line, group).wait_recv()
+            summed = summed + part_in[at, rows, :].astype(jnp.float32)
+        attn_all[mp, rows, :] = summed.astype(jnp.bfloat16)
+        attn_copy(mp, 0, group, core).start()
+        attn_copy(mp, 1, group, across).start()
+
+    def pass_on(group):
+        attn_copy(x_mp, 1, group, across).wait_recv()
+        attn_copy(x_mp, 2, group, core).start()
+
+    def finish(group):
+        rows = pl.ds(group * GROUP, GROUP)
+        attn_copy(core_mp, 0, group, core).wait_recv()
+        attn_copy(far_mp, 2, group, core).wait_recv()
+        attn = jnp.concatenate([attn_all[part, rows, :].astype(jnp.float32) for part in range(4)], axis=1)
+        gate = jnp.concatenate([u_all[part, rows, :].astype(jnp.float32) for part in range(4)], axis=1)
+        centred = attn - jnp.mean(attn, axis=1, keepdims=True)
+        variance = jnp.mean(centred * centred, axis=1, keepdims=True)
+        hidden = (centred * lax.rsqrt(variance + EPS) * gate).astype(jnp.bfloat16)
+        mixed = own_rows[rows, :]
+        for part in range(4):
+            mixed = mixed + jnp.dot(
+                hidden[:, part * width : (part + 1) * width],
+                wo_all[part],
+                preferred_element_type=jnp.float32,
+            )
+        out[rows, :] = mixed.astype(jnp.bfloat16)
+
+    @pl.loop(0, groups + 2)
+    def _(turn):
+        @pl.when(turn < groups)
+        def _():
+            collect(turn)
+
+        @pl.when((turn >= 1) & (turn < groups + 1))
+        def _():
+            pass_on(turn - 1)
+
+        @pl.when(turn >= 2)
+        def _():
+            finish(turn - 2)
+
+    @pl.loop(1, shards)
+    def _(step):
+        row_copy(me, (me + step) % shards).wait_send()
+
+    @pl.loop(0, shards)
+    def _(source):
+        core_copy(source).wait_send()
+        x_copy(source).wait_send()
+        fwd_copy(source).wait_send()
+
+    keys_copy.wait_send()
+    values_copy.wait_send()
+    for step in range(1, lines):
+        count_copy(line, (line + step) % lines).wait_send()
+    for step in range(1, 4):
+        out_weight_copy(mp, (mp + step) % 4).wait_send()
+    part_copy(u_all, mp, u_sems, 0, core).wait_send()
+    part_copy(u_all, mp, u_sems, 1, across).wait_send()
+    part_copy(u_all, x_mp, u_sems, 2, core).wait_send()
+
+    @pl.loop(0, groups)
+    def _(group):
+        for step in range(1, lines):
+            q_copy(line, (line + step) % lines, group).wait_send()
+            p_copy(line, (line + step) % lines, group).wait_send()
+        attn_copy(mp, 0, group, core).wait_send()
+        attn_copy(mp, 1, group, across).wait_send()
+        attn_copy(x_mp, 2, group, core).wait_send()
+
+
+def move_queries(
+    cand_feats, cand_perm, w_in, w_out, cache_k, cache_v, hist_len, hist_home, hist_slot, hist_mask
+):
+    shards = lax.axis_size("req")
+    cands, width = cand_feats.shape
+    full = w_in.shape[0]
+    lines = shards // 2
+    groups = cands // GROUP
+    keys = 2 * (MAXBLK // shards) * BLK
+    lengths = jnp.clip(hist_len[0] - BLK * jnp.arange(MAXBLK, dtype=jnp.int32), 0, BLK)
+    counts = jnp.pad((hist_mask[0] * lengths[None, :]).astype(jnp.float32), ((0, 8 - groups), (0, 0)))
+    bf16, f32 = jnp.bfloat16, jnp.float32
+    vmem = pl.BlockSpec(memory_space=pltpu.VMEM)
+    smem = pl.BlockSpec(memory_space=pltpu.SMEM)
+    pairs = [shards, shards, shards, shards, 2, lines, 4, lines * groups, lines * groups, 3, 3 * groups]
+    return pl.pallas_call(
+        functools.partial(kernel, shards),
+        out_shape=jax.ShapeDtypeStruct((cands, width), bf16),
+        in_specs=[vmem] * 7 + [smem] * 2,
+        out_specs=vmem,
+        scratch_shapes=[
+            pltpu.VMEM((4, cands, width), bf16),
+            pltpu.VMEM((cands, full), bf16),
+            pltpu.VMEM((cands, width), f32),
+            pltpu.VMEM((lines, cands, width), bf16),
+            pltpu.VMEM((4, cands, width), bf16),
+            pltpu.VMEM((cands, width), bf16),
+            pltpu.VMEM((cands, width), bf16),
+            pltpu.VMEM((4, width, width), bf16),
+            pltpu.VMEM(cache_k.shape, bf16),
+            pltpu.VMEM(cache_v.shape, bf16),
+            pltpu.VMEM((lines, 8, MAXBLK), f32),
+            pltpu.VMEM((lines, keys, width), bf16),
+            pltpu.VMEM((lines, keys, width), bf16),
+            pltpu.VMEM((lines, 8, keys), f32),
+            pltpu.VMEM((lines, cands, width), bf16),
+            pltpu.VMEM((lines, cands, width), bf16),
+            pltpu.VMEM((cands, width), f32),
+            pltpu.VMEM((4, cands, width), bf16),
+        ]
+        + [pltpu.SemaphoreType.DMA((count,)) for count in pairs for _ in range(2)],
+        compiler_params=pltpu.CompilerParams(
+            collective_id=0, has_side_effects=True, vmem_limit_bytes=48 * 1024 * 1024
+        ),
+        cost_estimate=pl.CostEstimate(flops=8 * 10**9, bytes_accessed=2**23, transcendentals=2**22),
+    )(
+        cand_feats.reshape(shards, cands // shards, width),
+        cand_perm.reshape(cands, 1),
+        w_in.transpose(1, 0, 2),
+        w_out,
+        cache_k,
+        cache_v,
+        counts,
+        hist_home,
+        hist_slot,
+    )
+
+
+def local(cand_feats, cand_perm, w_in, *rest):
+    shards = lax.axis_size("req")
+    shard_keys = MAXBLK // shards * BLK
+    queries_fit = cand_perm.shape[1] <= shard_keys and shards % 2 == 0
+    plan = move_queries if queries_fit and lax.axis_size("mp") == 4 else move_blocks
+    return plan(cand_feats, cand_perm, w_in, *rest)
+
+
 def solution(mesh):
     in_specs = (
         P("req", "mp"),

time: 194 us -> 78.9 us (0.41)
  waiting for transfers between devices: 88.6 us -> 0 us
  Pallas kernels: 0 us -> 72.9 us
  matrix products: 21.9 us -> 0 us
  local copies, waits for them, and re-layouts: 24.6 us -> 3.56 us
  starting transfers between devices: 17.6 us -> 0 us
  between operations: 14.3 us -> 0.77 us
  blocking collectives: 13.1 us -> 0 us
  other arithmetic: 12.8 us -> 0.7 us
    pallas_call x0 -> x1, Pallas kernels: none -> 72.9 us  [move_queries(): pl.pallas_call(functools.partial(kernel, shards), out_shape=jax.ShapeDtyp...]
    all_to_all x3 -> x0, waiting for transfers between devices: 57.6 us -> none  [the longest x1 43.9 us: local(): lax.all_to_all(send_keys, 'req', split_axis=0, concat_axis=0, tiled=True)]
    reduce_scatter x1 -> x0, waiting for transfers between devices: 31 us -> none  [local(): lax.psum_scatter(lax.dot_general(w_out, hidden, (((0,), (1,)), ((), ())),...]
    dot_general x6 -> x0, matrix products: 21.9 us -> none  [the longest x2 10 us: local(): lax.dot_general(q_head, hist_keys[:, lo_col:lo_col + DH], (((1,), (1,)),...]
    all_to_all x3 -> x0, starting transfers between devices: 17.3 us -> none  [the longest x1 6.51 us: local(): lax.all_to_all(cand_feats.reshape(shards, cand_slot, columns), 'req', spl...]
    psum x2 -> x0, blocking collectives: 13.1 us -> none  [the longest x1 7.3 us: local(): row_total = lax.psum(jnp.sum(attn, axis=1, keepdims=True), 'mp')]
    gather x8 -> x0, local copies, waits for them, and re-layouts: 10.4 us -> none  [the longest x1 2.45 us: local(): hist_values = got_values[source, round_at].reshape(key_count, local_width)]
    unnamed x29 -> x14, local copies, waits for them, and re-layouts: 8.9 us -> 2.73 us
  transfers between devices with their start and end apart: 5 -> 0, of which waited for: 3 -> 0; matrix products, arithmetic and copies ran while one was open for 23% -> 0% of each run, Pallas kernels for 0% -> 0%
where the time goes in v1:
time: 78.9 us; the launch traced here: 78 us
  Pallas kernels  72.9 us (92%)
  local copies, waits for them, and re-layouts  3.56 us (5%)
    pallas_call x1, Pallas kernels, move_queries(): pl.pallas_call(functools.partial(kernel, shards), out_shape=jax.ShapeDtyp...  72.9 us
    unnamed x14, local copies, waits for them, and re-layouts  2.73 us

profile of v1, /device:TPU:1, one launch (start us, length us, event | category | flops | bytes accessed | tf_op | source)
XLA Modules:
  0.0 78.0 jit_solution(15734859251842768599)
XLA Ops:
  0.7 0.7 fusion
  1.4 0.8 %copy.13.perm = s32[512,1]{1,0:T(8,128)S(1)} copy(s32[512,1]{0,1:T(1,128)} %bitcast.13) | data formatting | bytes 4096 | tf_op jit(solution)/shard_map/reshape | solution.py:585
  2.2 0.0 copy-start
  2.2 0.0 copy-start.1
  2.2 0.0 copy-start.2
  2.2 0.0 copy-start.3
  2.2 0.0 copy-start.4
  2.2 0.0 copy-start.5
  2.3 2.0 %copy.15 = bf16[1024,4,256]{2,0,1:T(8,128)(2,1)S(1)} copy(bf16[1024,4,256]{2,1,0:T(4,128)(2,1)} %param.12) | data formatting | bytes 4194304 | tf_op args[2]
  4.3 0.0 copy-done
  4.3 0.0 copy-done.1
  4.3 0.0 copy-done.2
  4.3 0.0 copy-done.3
  4.3 0.0 copy-done.4
  4.3 0.0 copy-done.5
  4.3 72.9 %shard_map.100 = bf16[512,256]{1,0:T(8,128)(2,1)S(1)} custom-call(bf16[8,64,256]{2,1,0:T(8,128)(2,1)S(1)} %bitcast.12, s32[512,1]{1,0:T(8,128)S(1)} %copy.13.perm, bf16[4,1024,256]{2,1,0:T(8,128)(2,1)S(1)} %bitcast.11, bf16[256,1024]{1,0:T(8,128)(2,1)S(1)} %copy-done, bf16[32,32,256]{2,1,0:T(8,128)(2,1)S(1)} %copy-done.1, ...), custom_call_target="tpu_custom_call" | custom-call | flops 8000000000 | bytes 8388608 | tf_op jit(solution)/shard_map/pallas_call | solution.py:553
  77.3 0.7 copy.18
  (2 shorter events, 0.0 us)
Async XLA Ops:
  2.2 2.1 %copy-start = (bf16[256,1024]{1,0:T(8,128)(2,1)S(1)}, bf16[256,1024]{1,0:T(8,128)(2,1)}, u32[]{:S(2)}) copy-start(bf16[256,1024]{1,0:T(8,128)(2,1)} %w_out.1) | copy-start | bytes 1572868
  2.2 2.1 %copy-start.1 = (bf16[32,32,256]{2,1,0:T(8,128)(2,1)S(1)}, bf16[32,32,256]{2,1,0:T(8,128)(2,1)}, u32[]{:S(2)}) copy-start(bf16[32,32,256]{2,1,0:T(8,128)(2,1)} %cache_k.1) | copy-start | bytes 1572868
  2.2 2.1 %copy-start.2 = (bf16[32,32,256]{2,1,0:T(8,128)(2,1)S(1)}, bf16[32,32,256]{2,1,0:T(8,128)(2,1)}, u32[]{:S(2)}) copy-start(bf16[32,32,256]{2,1,0:T(8,128)(2,1)} %cache_v.1) | copy-start | bytes 1572868
  2.2 2.1 %copy-start.3 = (bf16[512,256]{1,0:T(8,128)(2,1)S(1)}, bf16[512,256]{1,0:T(8,128)(2,1)}, u32[]{:S(2)}) copy-start(bf16[512,256]{1,0:T(8,128)(2,1)} %param.10) | copy-start | bytes 786436
  2.2 2.1 %copy-start.4 = (s32[8,128]{1,0:T(8,128)S(1)}, s32[8,128]{1,0:T(8,128)}, u32[]{:S(2)}) copy-start(s32[8,128]{1,0:T(8,128)} %slot.1) | copy-start | bytes 12292
  2.2 2.1 %copy-start.5 = (s32[8]{0:T(128)S(1)}, s32[8]{0:T(128)}, u32[]{:S(2)}) copy-start(s32[8]{0:T(128)} %home.1) | copy-start | bytes 100

commit v2 on v1

--- a/solution.py
+++ b/solution.py
@@ -145,10 +145,13 @@
     w_out,
     cache_k,
     cache_v,
-    counts,
+    block_mask,
+    length,
     home,
     slot,
     out,
+    w_parts,
+    counts,
     rows_all,
     normed,
     own_rows,
@@ -165,6 +168,7 @@
     mask,
     part_out,
     part_in,
+    part_own,
     total,
     attn_all,
     row_s,
@@ -194,6 +198,8 @@
     mp = lax.axis_index("mp")
     lines = shards // 2
     line, side = me // 2, me % 2
+    lines_by_distance = (line, line + 1 - 2 * (line % 2), (line + 2) % 4, 3 - line)
+    others = [(side + turn) % 2 + 2 * at for at in lines_by_distance for turn in range(2)][1:]
     mate = line * 2 + (1 - side)
     core_mp = (mp // 2) * 2 + (1 - mp % 2)
     x_mp = (1 - mp // 2) * 2 + mp % 2
@@ -268,10 +274,12 @@
     keys_copy = remote(cache_k, other_k, kv_s.at[0], kv_r.at[0], side_mate)
     values_copy = remote(cache_v, other_v, kv_s.at[1], kv_r.at[1], side_mate)
 
-    @pl.loop(1, shards)
-    def _(step):
-        row_copy(me, (me + step) % shards).start()
-
+    for target in others[::-1]:
+        row_copy(me, target).start()
+
+    places = lax.broadcasted_iota(jnp.int32, (groups, MAXBLK), 1) * BLK
+    counts[...] = jnp.zeros_like(counts)
+    counts[0:groups, :] = (block_mask[0] * jnp.clip(length[0] - places, 0, BLK)).astype(jnp.float32)
     for step in range(1, lines):
         count_copy(line, (line + step) % lines).start()
     keys_copy.start()
@@ -281,9 +289,13 @@
     core_copy(me).start()
     x_copy(me).start()
 
-    @pl.loop(1, shards)
-    def _(step):
-        source = (me + step) % shards
+    @pl.loop(0, w_in.shape[0], step=GROUP)
+    def _(first):
+        rows = pl.ds(pl.multiple_of(first, GROUP), GROUP)
+        for part in range(4):
+            w_parts[part, rows, :] = w_in[rows, part, :]
+
+    for source in others:
         row_copy(source, me).wait_recv()
         core_copy(source).start()
         x_copy(source).start()
@@ -307,9 +319,7 @@
 
     gather(cache_k, cache_v, me, 0)
 
-    @pl.loop(0, shards)
-    def _(step):
-        source = (me + step) % shards
+    for source in [me] + others:
         x_got(source).wait_recv()
         fwd_copy(source).start()
 
@@ -331,33 +341,34 @@
                 place.astype(jnp.float32) < live, 0.5 * DH ** (-0.5), 0.0
             )
 
-    @pl.loop(0, shards)
-    def _(step):
-        source = (me + step) % shards
+    for source in [me] + others:
         core_got(source).wait_recv()
         fwd_got(source).wait_recv()
 
-    def q_copy(source, target, group):
+
+    def q_copy(source, device_line, group, index):
         rows = pl.ds(group * GROUP, GROUP)
         return remote(
             q_all.at[source, rows],
             q_all.at[source, rows],
-            q_s.at[target * groups + group],
+            q_s.at[index * groups + group],
             q_r.at[source * groups + group],
-            (target * 2 + side, mp),
-        )
+            (device_line * 2 + side, mp),
+        )
+
+    below, above = line > 0, line < lines - 1
 
     def project(part, group):
         rows = pl.ds(group * GROUP, GROUP)
-        scores = jnp.dot(normed[rows, :], w_in[part], preferred_element_type=jnp.float32)
+        scores = jnp.dot(normed[rows, :], w_parts[part], preferred_element_type=jnp.float32)
         return half_silu(0.5 * scores).astype(jnp.bfloat16)
 
     @pl.loop(0, groups)
     def _(group):
         rows = pl.ds(group * GROUP, GROUP)
-        wanted = perm[rows, :]
-        pick = (lax.broadcasted_iota(jnp.int32, (GROUP, cands), 1) == wanted).astype(jnp.float32)
-        pick = pick.astype(jnp.bfloat16)
+        wanted = perm[:, pl.ds(pl.multiple_of(group * GROUP, GROUP), GROUP)]
+        chosen = lax.broadcasted_iota(jnp.int32, (cands, GROUP), 0) == wanted
+        pick = jnp.transpose(chosen.astype(jnp.float32)).astype(jnp.bfloat16)
         features = jnp.concatenate(
             [jnp.dot(pick, rows_all[part], preferred_element_type=jnp.float32) for part in range(4)],
             axis=1,
@@ -367,8 +378,14 @@
         variance = jnp.mean(centred * centred, axis=1, keepdims=True)
         normed[rows, :] = (centred * lax.rsqrt(variance + EPS)).astype(jnp.bfloat16)
         q_all[line, rows, :] = project(2, group)
-        for step in range(1, lines):
-            q_copy(line, (line + step) % lines, group).start()
+
+        @pl.when(above)
+        def _():
+            q_copy(line, line + 1, group, line).start()
+
+        @pl.when(below)
+        def _():
+            q_copy(line, line - 1, group, lines).start()
 
     @pl.loop(0, groups)
     def _(group):
@@ -416,23 +433,81 @@
             heads.append(summed)
         return jnp.concatenate(heads, axis=1)
 
-    def p_copy(source, target, group):
+    def p_copy(target, nearer, place, group):
         rows = pl.ds(group * GROUP, GROUP)
         return remote(
             part_out.at[target, rows],
-            part_in.at[source, rows],
+            part_in.at[place, rows],
             p_s.at[target * groups + group],
-            p_r.at[source * groups + group],
-            (target * 2 + side, mp),
-        )
-
-    @pl.loop(0, groups)
-    def _(group):
-        for step in range(1, lines):
-            at = (line + step) % lines
-            q_copy(at, line, group).wait_recv()
-            part_out[at, pl.ds(group * GROUP, GROUP), :] = attend(at, group).astype(jnp.bfloat16)
-            p_copy(line, at, group).start()
+            p_r.at[place * groups + group],
+            (nearer * 2 + side, mp),
+        )
+
+    def send_part(target, group):
+        rows = pl.ds(group * GROUP, GROUP)
+
+        @pl.when(target > line)
+        def _():
+            p_copy(target, line + 1, target, group).start()
+
+        @pl.when(target < line - 1)
+        def _():
+            p_copy(target, line - 1, target, group).start()
+
+        @pl.when(target == line - 1)
+        def _():
+            p_copy(target, line - 1, lines, group).start()
+
+    def visit(at, onward, group):
+        rows = pl.ds(group * GROUP, GROUP)
+        last = (onward < 0) | (onward >= lines)
+        q_copy(at, line, group, at).wait_recv()
+
+        @pl.when(jnp.logical_not(last))
+        def _():
+            q_copy(at, onward, group, at).start()
+
+        found = attend(at, group)
+
+        @pl.when(last)
+        def _():
+            part_out[at, rows, :] = found.astype(jnp.bfloat16)
+            send_part(at, group)
+
+        @pl.when(jnp.logical_not(last))
+        def _():
+            part_own[at, rows, :] = found
+
+    for distance in range(1, lines):
+
+        @pl.loop(0, groups)
+        def _(group):
+            @pl.when(line + distance < lines)
+            def _():
+                visit(line + distance, line - 1, group)
+
+            @pl.when(line - distance >= 0)
+            def _():
+                visit(line - distance, line + 1, group)
+
+    def relay(turn):
+        inner = (2, 3, 0)[turn]
+        at = jnp.where(line == 1, inner, 3 - inner)
+
+        @pl.loop(0, groups)
+        def _(group):
+            rows = pl.ds(group * GROUP, GROUP)
+            p_copy(at, line, at, group).wait_recv()
+            part_out[at, rows, :] = (
+                part_own[at, rows, :] + part_in[at, rows, :].astype(jnp.float32)
+            ).astype(jnp.bfloat16)
+            send_part(at, group)
+
+    @pl.when(above & below)
+    def _():
+        relay(0)
+        relay(1)
+        relay(2)
 
     part_copy(u_all, x_mp, u_sems, 1, across).wait_recv()
     part_copy(u_all, x_mp, u_sems, 2, core).start()
@@ -460,12 +535,18 @@
 
     def collect(group):
         rows = pl.ds(group * GROUP, GROUP)
-        summed = total[rows, :]
-        for step in range(1, lines):
-            at = (line + step) % lines
-            p_copy(at, line, group).wait_recv()
-            summed = summed + part_in[at, rows, :].astype(jnp.float32)
-        attn_all[mp, rows, :] = summed.astype(jnp.bfloat16)
+
+        @pl.when(below)
+        def _():
+            p_copy(line, line, line, group).wait_recv()
+            total[rows, :] += part_in[line, rows, :].astype(jnp.float32)
+
+        @pl.when(above)
+        def _():
+            p_copy(line, line, lines, group).wait_recv()
+            total[rows, :] += part_in[lines, rows, :].astype(jnp.float32)
+
+        attn_all[mp, rows, :] = total[rows, :].astype(jnp.bfloat16)
         attn_copy(mp, 0, group, core).start()
         attn_copy(mp, 1, group, across).start()
 
@@ -505,9 +586,8 @@
         def _():
             finish(turn - 2)
 
-    @pl.loop(1, shards)
-    def _(step):
-        row_copy(me, (me + step) % shards).wait_send()
+    for target in others:
+        row_copy(me, target).wait_send()
 
     @pl.loop(0, shards)
     def _(source):
@@ -528,8 +608,21 @@
     @pl.loop(0, groups)
     def _(group):
         for step in range(1, lines):
-            q_copy(line, (line + step) % lines, group).wait_send()
-            p_copy(line, (line + step) % lines, group).wait_send()
+            at = (line + step) % lines
+            p_copy(at, line, at, group).wait_send()
+
+            @pl.when(jnp.where(at > line, below, above))
+            def _():
+                q_copy(at, line, group, at).wait_send()
+
+        @pl.when(above)
+        def _():
+            q_copy(line, line, group, line).wait_send()
+
+        @pl.when(below)
+        def _():
+            q_copy(line, line, group, lines).wait_send()
+
         attn_copy(mp, 0, group, core).wait_send()
         attn_copy(mp, 1, group, across).wait_send()
         attn_copy(x_mp, 2, group, core).wait_send()
@@ -544,18 +637,19 @@
     lines = shards // 2
     groups = cands // GROUP
     keys = 2 * (MAXBLK // shards) * BLK
-    lengths = jnp.clip(hist_len[0] - BLK * jnp.arange(MAXBLK, dtype=jnp.int32), 0, BLK)
-    counts = jnp.pad((hist_mask[0] * lengths[None, :]).astype(jnp.float32), ((0, 8 - groups), (0, 0)))
     bf16, f32 = jnp.bfloat16, jnp.float32
     vmem = pl.BlockSpec(memory_space=pltpu.VMEM)
     smem = pl.BlockSpec(memory_space=pltpu.SMEM)
-    pairs = [shards, shards, shards, shards, 2, lines, 4, lines * groups, lines * groups, 3, 3 * groups]
+    lots = (lines + 1) * groups
+    pairs = [shards, shards, shards, shards, 2, lines, 4, lots, lots, 3, 3 * groups]
     return pl.pallas_call(
         functools.partial(kernel, shards),
         out_shape=jax.ShapeDtypeStruct((cands, width), bf16),
-        in_specs=[vmem] * 7 + [smem] * 2,
+        in_specs=[vmem] * 7 + [smem] * 3,
         out_specs=vmem,
         scratch_shapes=[
+            pltpu.VMEM((4, full, width), bf16),
+            pltpu.VMEM((8, MAXBLK), f32),
             pltpu.VMEM((4, cands, width), bf16),
             pltpu.VMEM((cands, full), bf16),
             pltpu.VMEM((cands, width), f32),
@@ -571,7 +665,8 @@
             pltpu.VMEM((lines, keys, width), bf16),
             pltpu.VMEM((lines, 8, keys), f32),
             pltpu.VMEM((lines, cands, width), bf16),
-            pltpu.VMEM((lines, cands, width), bf16),
+            pltpu.VMEM((lines + 1, cands, width), bf16),
+            pltpu.VMEM((lines, cands, width), f32),
             pltpu.VMEM((cands, width), f32),
             pltpu.VMEM((4, cands, width), bf16),
         ]
@@ -582,12 +677,13 @@
         cost_estimate=pl.CostEstimate(flops=8 * 10**9, bytes_accessed=2**23, transcendentals=2**22),
     )(
         cand_feats.reshape(shards, cands // shards, width),
-        cand_perm.reshape(cands, 1),
-        w_in.transpose(1, 0, 2),
+        cand_perm,
+        w_in,
         w_out,
         cache_k,
         cache_v,
-        counts,
+        hist_mask,
+        hist_len,
         hist_home,
         hist_slot,
     )
@@ -596,7 +692,7 @@
 def local(cand_feats, cand_perm, w_in, *rest):
     shards = lax.axis_size("req")
     shard_keys = MAXBLK // shards * BLK
-    queries_fit = cand_perm.shape[1] <= shard_keys and shards % 2 == 0
+    queries_fit = cand_perm.shape[1] <= shard_keys and shards == 8
     plan = move_queries if queries_fit and lax.axis_size("mp") == 4 else move_blocks
     return plan(cand_feats, cand_perm, w_in, *rest)
 

time: 78.9 us -> 79.8 us (1.011)
  local copies, waits for them, and re-layouts: 3.56 us -> 9.07 us
  Pallas kernels: 72.9 us -> 68.8 us
    unnamed x14 -> x19, local copies, waits for them, and re-layouts: 2.73 us -> 9.07 us
    pallas_call x1, Pallas kernels: 72.9 us -> 68.8 us  [move_queries(): pl.pallas_call(functools.partial(kernel, shards), out_shape=jax.ShapeDtyp...]
    reshape x1 -> x0, local copies, waits for them, and re-layouts: 0.82 us -> none  [move_queries(): cand_perm.reshape(cands, 1)]
where the time goes in v2:
time: 79.8 us; the launch traced here: 78.5 us
  Pallas kernels  68.8 us (86%)
  local copies, waits for them, and re-layouts  9.07 us (11%)
    pallas_call x1, Pallas kernels, move_queries(): pl.pallas_call(functools.partial(kernel, shards), out_shape=jax.ShapeDtyp...  68.8 us
    unnamed x19, local copies, waits for them, and re-layouts  9.07 us

profile of v2, /device:TPU:1, one launch (start us, length us, event | category | flops | bytes accessed | tf_op | source)
XLA Modules:
  0.0 78.5 jit_solution(11501346184217648318)
XLA Ops:
  0.7 0.0 copy-start
  0.7 1.6 %copy-done = bf16[1024,4,256]{2,1,0:T(4,128)(2,1)S(1)} copy-done((bf16[1024,4,256]{2,1,0:T(4,128)(2,1)S(1)}, bf16[1024,4,256]{2,1,0:T(4,128)(2,1)}, u32[]{:S(2)}) %copy-start) | copy-done | bytes 2097176
  2.2 0.0 copy-start.1
  2.2 1.0 %copy-done.1 = bf16[256,1024]{1,0:T(8,128)(2,1)S(1)} copy-done((bf16[256,1024]{1,0:T(8,128)(2,1)S(1)}, bf16[256,1024]{1,0:T(8,128)(2,1)}, u32[]{:S(2)}) %copy-start.1) | copy-done | bytes 524312
  3.3 0.0 copy-start.2
  3.3 1.0 %copy-done.2 = bf16[32,32,256]{2,1,0:T(8,128)(2,1)S(1)} copy-done((bf16[32,32,256]{2,1,0:T(8,128)(2,1)S(1)}, bf16[32,32,256]{2,1,0:T(8,128)(2,1)}, u32[]{:S(2)}) %copy-start.2) | copy-done | bytes 524312
  4.3 0.0 copy-start.3
  4.3 1.0 %copy-done.3 = bf16[32,32,256]{2,1,0:T(8,128)(2,1)S(1)} copy-done((bf16[32,32,256]{2,1,0:T(8,128)(2,1)S(1)}, bf16[32,32,256]{2,1,0:T(8,128)(2,1)}, u32[]{:S(2)}) %copy-start.3) | copy-done | bytes 524312
  5.4 0.0 copy-start.4
  5.4 0.9 %copy-done.4 = bf16[512,256]{1,0:T(8,128)(2,1)S(1)} copy-done((bf16[512,256]{1,0:T(8,128)(2,1)S(1)}, bf16[512,256]{1,0:T(8,128)(2,1)}, u32[]{:S(2)}) %copy-start.4) | copy-done | bytes 262168
  6.3 0.0 copy-start.5
  6.3 0.7 copy-done.5
  7.0 0.0 copy-start.6
  7.0 0.7 copy-done.6
  7.7 0.0 copy-start.7
  7.7 0.7 copy-done.7
  8.4 0.0 copy-start.8
  8.4 0.7 copy-done.8
  9.0 68.8 %shard_map.100 = bf16[512,256]{1,0:T(8,128)(2,1)S(1)} custom-call(bf16[8,64,256]{2,1,0:T(8,128)(2,1)S(1)} %bitcast.1, s32[1,512]{1,0:T(1,128)S(1)} %copy-done.6, bf16[1024,4,256]{2,1,0:T(4,128)(2,1)S(1)} %copy-done, bf16[256,1024]{1,0:T(8,128)(2,1)S(1)} %copy-done.1, bf16[32,32,256]{2,1,0:T(8,128)(2,1)S(1)} %copy-done.2, bf16[32,32,256]{2,1,0:T(8,128)(2,1)S(1)} %copy-done.3, ...), custom_call_target="tpu_custom_call" | custom-call | flops 8000000000 | bytes 8388608 | tf_op jit(solution)/shard_map/pallas_call | solution.py:645
  77.8 0.7 copy.13
Async XLA Ops:
  0.7 1.6 %copy-start = (bf16[1024,4,256]{2,1,0:T(4,128)(2,1)S(1)}, bf16[1024,4,256]{2,1,0:T(4,128)(2,1)}, u32[]{:S(2)}) copy-start(bf16[1024,4,256]{2,1,0:T(4,128)(2,1)} %w_in.1) | copy-start | bytes 6291460
  2.2 1.0 %copy-start.1 = (bf16[256,1024]{1,0:T(8,128)(2,1)S(1)}, bf16[256,1024]{1,0:T(8,128)(2,1)}, u32[]{:S(2)}) copy-start(bf16[256,1024]{1,0:T(8,128)(2,1)} %w_out.1) | copy-start | bytes 1572868
  3.3 1.0 %copy-start.2 = (bf16[32,32,256]{2,1,0:T(8,128)(2,1)S(1)}, bf16[32,32,256]{2,1,0:T(8,128)(2,1)}, u32[]{:S(2)}) copy-start(bf16[32,32,256]{2,1,0:T(8,128)(2,1)} %cache_k.1) | copy-start | bytes 1572868
  4.3 1.0 %copy-start.3 = (bf16[32,32,256]{2,1,0:T(8,128)(2,1)S(1)}, bf16[32,32,256]{2,1,0:T(8,128)(2,1)}, u32[]{:S(2)}) copy-start(bf16[32,32,256]{2,1,0:T(8,128)(2,1)} %cache_v.1) | copy-start | bytes 1572868
  5.4 0.9 %copy-start.4 = (bf16[512,256]{1,0:T(8,128)(2,1)S(1)}, bf16[512,256]{1,0:T(8,128)(2,1)}, u32[]{:S(2)}) copy-start(bf16[512,256]{1,0:T(8,128)(2,1)} %param.10) | copy-start | bytes 786436
  6.3 0.7 copy-start.5
  7.0 0.7 copy-start.6
  7.7 0.7 copy-start.7
  8.4 0.7 copy-start.8

commit v3 on v2

--- a/solution.py
+++ b/solution.py
@@ -137,21 +137,29 @@
     return half + half * jnp.tanh(half)
 
 
+SPAN = 256
+TILE = 256
+
+
 def kernel(
     shards,
     feats,
     perm,
-    w_in,
+    w_in_far,
     w_out,
-    cache_k,
-    cache_v,
+    cache_k_far,
+    cache_v_far,
     block_mask,
     length,
     home,
     slot,
     out,
+    w_in,
+    cache_k,
+    cache_v,
     w_parts,
     counts,
+    picked,
     rows_all,
     normed,
     own_rows,
@@ -193,6 +201,7 @@
     u_r,
     a_s,
     a_r,
+    in_s,
 ):
     me = lax.axis_index("req")
     mp = lax.axis_index("mp")
@@ -207,10 +216,25 @@
     slots = feats.shape[1]
     width = feats.shape[2]
     cands = shards * slots
-    groups = cands // GROUP
+    groups, pieces = cands // GROUP, cands // SPAN
     rounds = MAXBLK // shards
     keys_here = rounds * BLK
     core, across, side_mate = (me, core_mp), (me, x_mp), (mate, mp)
+
+    loads = [
+        pltpu.make_async_copy(far, near, in_s.at[index])
+        for index, (far, near) in enumerate(
+            (
+                (feats.at[me], rows_all.at[mp, pl.ds(me * slots, slots)]),
+                (w_in_far, w_in),
+                (cache_k_far, cache_k),
+                (cache_v_far, cache_v),
+                (w_out.at[:, pl.ds(pl.multiple_of(mp * width, width), width)], wo_all.at[mp]),
+            )
+        )
+    ]
+    for load in loads:
+        load.start()
 
     barrier = pltpu.get_barrier_semaphore()
     for step in range(1, shards):
@@ -271,8 +295,8 @@
             chunk(far_mp, source), chunk(far_mp, source), fwd_s.at[source], fwd_r.at[source], core
         )
 
-    keys_copy = remote(cache_k, other_k, kv_s.at[0], kv_r.at[0], side_mate)
-    values_copy = remote(cache_v, other_v, kv_s.at[1], kv_r.at[1], side_mate)
+    keys_copy = remote(cache_k_far, other_k, kv_s.at[0], kv_r.at[0], side_mate)
+    values_copy = remote(cache_v_far, other_v, kv_s.at[1], kv_r.at[1], side_mate)
 
     for target in others[::-1]:
         row_copy(me, target).start()
@@ -284,10 +308,12 @@
         count_copy(line, (line + step) % lines).start()
     keys_copy.start()
     values_copy.start()
-    rows_all[mp, pl.ds(me * slots, slots), :] = feats[me]
+    loads[0].wait()
     counts_all[line] = counts[...]
     core_copy(me).start()
     x_copy(me).start()
+
+    loads[1].wait()
 
     @pl.loop(0, w_in.shape[0], step=GROUP)
     def _(first):
@@ -302,7 +328,6 @@
 
     for step in range(1, 4):
         out_weight_copy(mp, (mp + step) % 4).start()
-    wo_all[mp] = w_out[:, pl.ds(pl.multiple_of(mp * width, width), width)]
 
     def gather(keys_ref, values_ref, shard, half):
         @pl.loop(0, lines)
@@ -313,10 +338,14 @@
             @pl.loop(0, rounds)
             def _(turn):
                 place = slot[request, first + turn * shards]
-                rows = pl.ds(half * keys_here + turn * BLK, BLK)
-                hist_k[at, rows, :] = keys_ref[place]
-                hist_v[at, rows, :] = values_ref[place]
-
+                picked[pl.ds(turn * BLK, BLK), :] = keys_ref[place]
+                hist_v[at, pl.ds(half * keys_here + turn * BLK, BLK), :] = values_ref[place]
+
+            hist_k[at, :, half * keys_here : (half + 1) * keys_here] = jnp.transpose(picked[...])
+
+    loads[2].wait()
+    loads[3].wait()
+    loads[4].wait()
     gather(cache_k, cache_v, me, 0)
 
     for source in [me] + others:
@@ -346,28 +375,28 @@
         fwd_got(source).wait_recv()
 
 
-    def q_copy(source, device_line, group, index):
-        rows = pl.ds(group * GROUP, GROUP)
+    def q_copy(source, device_line, piece, index):
+        rows = pl.ds(piece * SPAN, SPAN)
         return remote(
             q_all.at[source, rows],
             q_all.at[source, rows],
-            q_s.at[index * groups + group],
-            q_r.at[source * groups + group],
+            q_s.at[index * pieces + piece],
+            q_r.at[source * pieces + piece],
             (device_line * 2 + side, mp),
         )
 
     below, above = line > 0, line < lines - 1
 
-    def project(part, group):
-        rows = pl.ds(group * GROUP, GROUP)
+    def project(part, piece):
+        rows = pl.ds(piece * SPAN, SPAN)
         scores = jnp.dot(normed[rows, :], w_parts[part], preferred_element_type=jnp.float32)
         return half_silu(0.5 * scores).astype(jnp.bfloat16)
 
-    @pl.loop(0, groups)
-    def _(group):
-        rows = pl.ds(group * GROUP, GROUP)
-        wanted = perm[:, pl.ds(pl.multiple_of(group * GROUP, GROUP), GROUP)]
-        chosen = lax.broadcasted_iota(jnp.int32, (cands, GROUP), 0) == wanted
+    @pl.loop(0, pieces)
+    def _(piece):
+        rows = pl.ds(piece * SPAN, SPAN)
+        wanted = perm[:, pl.ds(pl.multiple_of(piece * SPAN, SPAN), SPAN)]
+        chosen = lax.broadcasted_iota(jnp.int32, (cands, SPAN), 0) == wanted
         pick = jnp.transpose(chosen.astype(jnp.float32)).astype(jnp.bfloat16)
         features = jnp.concatenate(
             [jnp.dot(pick, rows_all[part], preferred_element_type=jnp.float32) for part in range(4)],
@@ -377,19 +406,19 @@
         centred = features - jnp.mean(features, axis=1, keepdims=True)
         variance = jnp.mean(centred * centred, axis=1, keepdims=True)
         normed[rows, :] = (centred * lax.rsqrt(variance + EPS)).astype(jnp.bfloat16)
-        q_all[line, rows, :] = project(2, group)
+        q_all[line, rows, :] = project(2, piece)
 
         @pl.when(above)
         def _():
-            q_copy(line, line + 1, group, line).start()
+            q_copy(line, line + 1, piece, line).start()
 
         @pl.when(below)
         def _():
-            q_copy(line, line - 1, group, lines).start()
-
-    @pl.loop(0, groups)
-    def _(group):
-        u_all[mp, pl.ds(group * GROUP, GROUP), :] = project(0, group)
+            q_copy(line, line - 1, piece, lines).start()
+
+    @pl.loop(0, pieces)
+    def _(piece):
+        u_all[mp, pl.ds(piece * SPAN, SPAN), :] = project(0, piece)
 
     def part_copy(buffer, part, sems, index, device):
         send, receive = sems
@@ -399,80 +428,78 @@
     part_copy(u_all, mp, u_sems, 0, core).start()
     part_copy(u_all, mp, u_sems, 1, across).start()
 
-    @pl.loop(0, groups)
-    def _(group):
-        rows = pl.ds(group * GROUP, GROUP)
-        v_own[rows, :] = project(1, group)
-        k_own[rows, :] = project(3, group)
+    @pl.loop(0, pieces)
+    def _(piece):
+        rows = pl.ds(piece * SPAN, SPAN)
+        v_own[rows, :] = project(1, piece)
+        k_own[rows, :] = project(3, piece)
 
     keys_copy.wait_recv()
     values_copy.wait_recv()
     gather(other_k, other_v, mate, 1)
 
-    def attend(at, group):
-        rows = pl.ds(group * GROUP, GROUP)
-        scale = mask[at, pl.ds(group, 1), :]
+    def attend(at, piece):
+        rows = pl.ds(piece * SPAN, SPAN)
         heads = []
         for lo in range(0, width, DH):
             query = q_all[at, rows, lo : lo + DH]
             summed = None
-            for first in range(0, 2 * keys_here, keys_here):
-                scores = lax.dot_general(
-                    query,
-                    hist_k[at, first : first + keys_here, lo : lo + DH],
-                    (((1,), (1,)), ((), ())),
-                    preferred_element_type=jnp.float32,
-                )
-                weights = half_silu(scores * scale[:, first : first + keys_here]).astype(jnp.bfloat16)
+            for first in range(0, 2 * keys_here, TILE):
+                tile = slice(first, first + TILE)
+                scores = jnp.dot(query, hist_k[at, lo : lo + DH, tile], preferred_element_type=jnp.float32)
+                halves = [
+                    scores[at_row : at_row + GROUP]
+                    * mask[at, pl.ds(piece * (SPAN // GROUP) + at_row // GROUP, 1), tile]
+                    for at_row in range(0, SPAN, GROUP)
+                ]
+                weights = half_silu(jnp.concatenate(halves, axis=0).astype(jnp.bfloat16))
                 term = jnp.dot(
-                    weights,
-                    hist_v[at, first : first + keys_here, lo : lo + DH],
-                    preferred_element_type=jnp.float32,
+                    weights, hist_v[at, tile, lo : lo + DH], preferred_element_type=jnp.float32
                 )
                 summed = term if summed is None else summed + term
             heads.append(summed)
         return jnp.concatenate(heads, axis=1)
 
-    def p_copy(target, nearer, place, group):
-        rows = pl.ds(group * GROUP, GROUP)
+    def p_copy(target, nearer, place, piece):
+        rows = pl.ds(piece * SPAN, SPAN)
         return remote(
             part_out.at[target, rows],
             part_in.at[place, rows],
-            p_s.at[target * groups + group],
-            p_r.at[place * groups + group],
+            p_s.at[target * pieces + piece],
+            p_r.at[place * pieces + piece],
             (nearer * 2 + side, mp),
         )
 
-    def send_part(target, group):
-        rows = pl.ds(group * GROUP, GROUP)
+    def send_part(target, piece):
+        rows = pl.ds(piece * SPAN, SPAN)
 
         @pl.when(target > line)
         def _():
-            p_copy(target, line + 1, target, group).start()
+            p_copy(target, line + 1, target, piece).start()
 
         @pl.when(target < line - 1)
         def _():
-            p_copy(target, line - 1, target, group).start()
+            p_copy(target, line - 1, target, piece).start()
 
         @pl.when(target == line - 1)
         def _():
-            p_copy(target, line - 1, lines, group).start()
-
-    def visit(at, onward, group):
-        rows = pl.ds(group * GROUP, GROUP)
+            p_copy(target, line - 1, lines, piece).start()
+
+    def visit(at, onward, piece):
+        rows = pl.ds(piece * SPAN, SPAN)
         last = (onward < 0) | (onward >= lines)
-        q_copy(at, line, group, at).wait_recv()
+        q_copy(at, line, piece, at).wait_recv()
 
         @pl.when(jnp.logical_not(last))
         def _():
-            q_copy(at, onward, group, at).start()
-
-        found = attend(at, group)
+            q_copy(at, onward, piece, at).start()
+
+        found = attend(at, piece)
 
         @pl.when(last)
         def _():
             part_out[at, rows, :] = found.astype(jnp.bfloat16)
-            send_part(at, group)
+            send_part(at, piece)
 
         @pl.when(jnp.logical_not(last))
         def _():
@@ -480,84 +507,84 @@
 
     for distance in range(1, lines):
 
-        @pl.loop(0, groups)
-        def _(group):
+        @pl.loop(0, pieces)
+        def _(piece):
             @pl.when(line + distance < lines)
             def _():
-                visit(line + distance, line - 1, group)
+                visit(line + distance, line - 1, piece)
 
             @pl.when(line - distance >= 0)
             def _():
-                visit(line - distance, line + 1, group)
-
-    def relay(turn):
-        inner = (2, 3, 0)[turn]
-        at = jnp.where(line == 1, inner, 3 - inner)
-
-        @pl.loop(0, groups)
-        def _(group):
-            rows = pl.ds(group * GROUP, GROUP)
-            p_copy(at, line, at, group).wait_recv()
-            part_out[at, rows, :] = (
-                part_own[at, rows, :] + part_in[at, rows, :].astype(jnp.float32)
-            ).astype(jnp.bfloat16)
-            send_part(at, group)
-
-    @pl.when(above & below)
-    def _():
-        relay(0)
-        relay(1)
-        relay(2)
-
-    part_copy(u_all, x_mp, u_sems, 1, across).wait_recv()
-    part_copy(u_all, x_mp, u_sems, 2, core).start()
-
-    @pl.loop(0, groups)
-    def _(group):
-        rows = pl.ds(group * GROUP, GROUP)
+                visit(line - distance, line + 1, piece)
+
+    @pl.loop(0, pieces)
+    def _(piece):
+        rows = pl.ds(piece * SPAN, SPAN)
         own = []
         for lo in range(0, width, DH):
             query = q_all[line, rows, lo : lo + DH].astype(jnp.float32)
             key = k_own[rows, lo : lo + DH].astype(jnp.float32)
             half = jnp.sum(query * key, axis=1, keepdims=True) * (0.5 * DH ** (-0.5))
             own.append(half_silu(half) * v_own[rows, lo : lo + DH].astype(jnp.float32))
-        total[rows, :] = attend(line, group) + jnp.concatenate(own, axis=1)
+        total[rows, :] = attend(line, piece) + jnp.concatenate(own, axis=1)
+
+    def relay(turn):
+        inner = (2, 3, 0)[turn]
+        at = jnp.where(line == 1, inner, 3 - inner)
+
+        @pl.loop(0, pieces)
+        def _(piece):
+            rows = pl.ds(piece * SPAN, SPAN)
+            p_copy(at, line, at, piece).wait_recv()
+            part_out[at, rows, :] = (
+                part_own[at, rows, :] + part_in[at, rows, :].astype(jnp.float32)
+            ).astype(jnp.bfloat16)
+            send_part(at, piece)
+
+    @pl.when(above & below)
+    def _():
+        relay(0)
+        relay(1)
+        relay(2)
+
+    part_copy(u_all, x_mp, u_sems, 1, across).wait_recv()
+    part_copy(u_all, x_mp, u_sems, 2, core).start()
 
     part_copy(u_all, core_mp, u_sems, 0, core).wait_recv()
     part_copy(u_all, far_mp, u_sems, 2, core).wait_recv()
     for step in range(1, 4):
         out_weight_copy((mp + step) % 4, mp).wait_recv()
 
-    def attn_copy(part, kind, group, device):
-        piece = attn_all.at[part, pl.ds(group * GROUP, GROUP)]
-        index = kind * groups + group
-        return remote(piece, piece, a_s.at[index], a_r.at[index], device)
-
-    def collect(group):
-        rows = pl.ds(group * GROUP, GROUP)
+    def attn_copy(part, kind, piece, device):
+        block = attn_all.at[part, pl.ds(piece * SPAN, SPAN)]
+        index = kind * pieces + piece
+        return remote(block, block, a_s.at[index], a_r.at[index], device)
+
+    def collect(piece):
+        rows = pl.ds(piece * SPAN, SPAN)
 
         @pl.when(below)
         def _():
-            p_copy(line, line, line, group).wait_recv()
+            p_copy(line, line, line, piece).wait_recv()
             total[rows, :] += part_in[line, rows, :].astype(jnp.float32)
 
         @pl.when(above)
         def _():
-            p_copy(line, line, lines, group).wait_recv()
+            p_copy(line, line, lines, piece).wait_recv()
             total[rows, :] += part_in[lines, rows, :].astype(jnp.float32)
 
         attn_all[mp, rows, :] = total[rows, :].astype(jnp.bfloat16)
-        attn_copy(mp, 0, group, core).start()
-        attn_copy(mp, 1, group, across).start()
-
-    def pass_on(group):
-        attn_copy(x_mp, 1, group, across).wait_recv()
-        attn_copy(x_mp, 2, group, core).start()
-
-    def finish(group):
-        rows = pl.ds(group * GROUP, GROUP)
-        attn_copy(core_mp, 0, group, core).wait_recv()
-        attn_copy(far_mp, 2, group, core).wait_recv()
+        attn_copy(mp, 0, piece, core).start()
+        attn_copy(mp, 1, piece, across).start()
+
+    def pass_on(piece):
+        attn_copy(x_mp, 1, piece, across).wait_recv()
+        attn_copy(x_mp, 2, piece, core).start()
+
+    def finish(piece):
+        rows = pl.ds(piece * SPAN, SPAN)
+        attn_copy(core_mp, 0, piece, core).wait_recv()
+        attn_copy(far_mp, 2, piece, core).wait_recv()
         attn = jnp.concatenate([attn_all[part, rows, :].astype(jnp.float32) for part in range(4)], axis=1)
         gate = jnp.concatenate([u_all[part, rows, :].astype(jnp.float32) for part in range(4)], axis=1)
         centred = attn - jnp.mean(attn, axis=1, keepdims=True)
@@ -572,13 +599,13 @@
             )
         out[rows, :] = mixed.astype(jnp.bfloat16)
 
-    @pl.loop(0, groups + 2)
+    @pl.loop(0, pieces + 2)
     def _(turn):
-        @pl.when(turn < groups)
+        @pl.when(turn < pieces)
         def _():
             collect(turn)
 
-        @pl.when((turn >= 1) & (turn < groups + 1))
+        @pl.when((turn >= 1) & (turn < pieces + 1))
         def _():
             pass_on(turn - 1)
 
@@ -605,27 +632,27 @@
     part_copy(u_all, mp, u_sems, 1, across).wait_send()
     part_copy(u_all, x_mp, u_sems, 2, core).wait_send()
 
-    @pl.loop(0, groups)
-    def _(group):
+    @pl.loop(0, pieces)
+    def _(piece):
         for step in range(1, lines):
             at = (line + step) % lines
-            p_copy(at, line, at, group).wait_send()
+            p_copy(at, line, at, piece).wait_send()
 
             @pl.when(jnp.where(at > line, below, above))
             def _():
-                q_copy(at, line, group, at).wait_send()
+                q_copy(at, line, piece, at).wait_send()
 
         @pl.when(above)
         def _():
-            q_copy(line, line, group, line).wait_send()
+            q_copy(line, line, piece, line).wait_send()
 
         @pl.when(below)
         def _():
-            q_copy(line, line, group, lines).wait_send()
-
-        attn_copy(mp, 0, group, core).wait_send()
-        attn_copy(mp, 1, group, across).wait_send()
-        attn_copy(x_mp, 2, group, core).wait_send()
+            q_copy(line, line, piece, lines).wait_send()
+
+        attn_copy(mp, 0, piece, core).wait_send()
+        attn_copy(mp, 1, piece, across).wait_send()
+        attn_copy(x_mp, 2, piece, core).wait_send()
 
 
 def move_queries(
@@ -635,21 +662,26 @@
     cands, width = cand_feats.shape
     full = w_in.shape[0]
     lines = shards // 2
-    groups = cands // GROUP
+    pieces = cands // SPAN
     keys = 2 * (MAXBLK // shards) * BLK
     bf16, f32 = jnp.bfloat16, jnp.float32
     vmem = pl.BlockSpec(memory_space=pltpu.VMEM)
     smem = pl.BlockSpec(memory_space=pltpu.SMEM)
-    lots = (lines + 1) * groups
-    pairs = [shards, shards, shards, shards, 2, lines, 4, lots, lots, 3, 3 * groups]
+    far = pl.BlockSpec(memory_space=pl.ANY)
+    lots = (lines + 1) * pieces
+    pairs = [shards, shards, shards, shards, 2, lines, 4, lots, lots, 3, 3 * pieces]
     return pl.pallas_call(
         functools.partial(kernel, shards),
         out_shape=jax.ShapeDtypeStruct((cands, width), bf16),
-        in_specs=[vmem] * 7 + [smem] * 3,
+        in_specs=[far, vmem] + [far] * 4 + [vmem] + [smem] * 3,
         out_specs=vmem,
         scratch_shapes=[
+            pltpu.VMEM(w_in.shape, bf16),
+            pltpu.VMEM(cache_k.shape, bf16),
+            pltpu.VMEM(cache_v.shape, bf16),
             pltpu.VMEM((4, full, width), bf16),
             pltpu.VMEM((8, MAXBLK), f32),
+            pltpu.VMEM((keys // 2, width), bf16),
             pltpu.VMEM((4, cands, width), bf16),
             pltpu.VMEM((cands, full), bf16),
             pltpu.VMEM((cands, width), f32),
@@ -661,7 +693,7 @@
             pltpu.VMEM(cache_k.shape, bf16),
             pltpu.VMEM(cache_v.shape, bf16),
             pltpu.VMEM((lines, 8, MAXBLK), f32),
-            pltpu.VMEM((lines, keys, width), bf16),
+            pltpu.VMEM((lines, width, keys), bf16),
             pltpu.VMEM((lines, keys, width), bf16),
             pltpu.VMEM((lines, 8, keys), f32),
             pltpu.VMEM((lines, cands, width), bf16),
@@ -670,9 +702,10 @@
             pltpu.VMEM((cands, width), f32),
             pltpu.VMEM((4, cands, width), bf16),
         ]
-        + [pltpu.SemaphoreType.DMA((count,)) for count in pairs for _ in range(2)],
+        + [pltpu.SemaphoreType.DMA((count,)) for count in pairs for _ in range(2)]
+        + [pltpu.SemaphoreType.DMA((5,))],
         compiler_params=pltpu.CompilerParams(
-            collective_id=0, has_side_effects=True, vmem_limit_bytes=48 * 1024 * 1024
+            collective_id=0, has_side_effects=True, vmem_limit_bytes=56 * 1024 * 1024
         ),
         cost_estimate=pl.CostEstimate(flops=8 * 10**9, bytes_accessed=2**23, transcendentals=2**22),
     )(

time: 79.8 us -> 73.9 us (0.926); the launches traced: 78.5 us -> 73.7 us
  local copies, waits for them, and re-layouts: 9.07 us -> 1.67 us
  Pallas kernels: 68.8 us -> 71.4 us
    unnamed x19 -> x1, local copies, waits for them, and re-layouts: 9.07 us -> 1.67 us
    pallas_call x1, Pallas kernels: 68.8 us -> 71.4 us  [move_queries(): pl.pallas_call(functools.partial(kernel, shards), out_shape=jax.ShapeDtyp...]
where the time goes in v3:
time: 73.9 us; the launch traced here: 73.7 us
  Pallas kernels  71.4 us (97%)
  local copies, waits for them, and re-layouts  1.67 us (2%)
    pallas_call x1, Pallas kernels, move_queries(): pl.pallas_call(functools.partial(kernel, shards), out_shape=jax.ShapeDtyp...  71.4 us
    unnamed x1, local copies, waits for them, and re-layouts  1.67 us

profile of v3, /device:TPU:1, one launch (start us, length us, event | category | flops | bytes accessed | tf_op | source)
XLA Modules:
  0.0 73.7 jit_solution(7373114090363914176)
XLA Ops:
  0.7 71.4 %shard_map.100 = bf16[512,256]{1,0:T(8,128)(2,1)} custom-call(bf16[8,64,256]{2,1,0:T(8,128)(2,1)} %bitcast.1, s32[1,512]{1,0:T(1,128)} %perm.1, bf16[1024,4,256]{2,1,0:T(4,128)(2,1)} %w_in_far.1, bf16[256,1024]{1,0:T(8,128)(2,1)} %w_out.1, bf16[32,32,256]{2,1,0:T(8,128)(2,1)} %cache_k_far.1, bf16[32,32,256]{2,1,0:T(8,128)(2,1)} %cache_v_far.1, ...), custom_call_target="tpu_custom_call" | custom-call | flops 8000000000 | bytes 8388608 | tf_op jit(solution)/shard_map/pallas_call | solution.py:673
  72.0 1.7 %copy.13 = bf16[512,256]{1,0:T(8,128)(2,1)} copy(bf16[512,256]{1,0:T(8,128)(2,1)} %shard_map.100) | data formatting | bytes 524288

commit v4 on v3

--- a/solution.py
+++ b/solution.py
@@ -329,24 +329,23 @@
     for step in range(1, 4):
         out_weight_copy(mp, (mp + step) % 4).start()
 
-    def gather(keys_ref, values_ref, shard, half):
-        @pl.loop(0, lines)
-        def _(at):
-            request = at * 2 + side
-            first = lax.rem(shard - home[request] + shards, shards)
-
-            @pl.loop(0, rounds)
-            def _(turn):
-                place = slot[request, first + turn * shards]
-                picked[pl.ds(turn * BLK, BLK), :] = keys_ref[place]
-                hist_v[at, pl.ds(half * keys_here + turn * BLK, BLK), :] = values_ref[place]
-
-            hist_k[at, :, half * keys_here : (half + 1) * keys_here] = jnp.transpose(picked[...])
+    def gather(at, keys_ref, values_ref, shard, half):
+        request = at * 2 + side
+        first = lax.rem(shard - home[request] + shards, shards)
+        for turn in range(rounds):
+            place = slot[request, first + turn * shards]
+            picked[turn * BLK : (turn + 1) * BLK, :] = keys_ref[place]
+            begin = half * keys_here + turn * BLK
+            hist_v[at, begin : begin + BLK, :] = values_ref[place]
+        hist_k[at, :, half * keys_here : (half + 1) * keys_here] = jnp.transpose(picked[...])
 
     loads[2].wait()
     loads[3].wait()
     loads[4].wait()
-    gather(cache_k, cache_v, me, 0)
+
+    @pl.loop(0, lines)
+    def _(at):
+        gather(at, cache_k, cache_v, me, 0)
 
     for source in [me] + others:
         x_got(source).wait_recv()
@@ -434,17 +433,13 @@
         v_own[rows, :] = project(1, piece)
         k_own[rows, :] = project(3, piece)
 
-    keys_copy.wait_recv()
-    values_copy.wait_recv()
-    gather(other_k, other_v, mate, 1)
-
-    def attend(at, piece):
+    def attend(at, piece, half):
         rows = pl.ds(piece * SPAN, SPAN)
         heads = []
         for lo in range(0, width, DH):
             query = q_all[at, rows, lo : lo + DH]
             summed = None
-            for first in range(0, 2 * keys_here, TILE):
+            for first in range(half * keys_here, (half + 1) * keys_here, TILE):
                 tile = slice(first, first + TILE)
                 scores = jnp.dot(query, hist_k[at, lo : lo + DH, tile], preferred_element_type=jnp.float32)
                 halves = [
@@ -487,35 +482,13 @@
 
     def visit(at, onward, piece):
         rows = pl.ds(piece * SPAN, SPAN)
-        last = (onward < 0) | (onward >= lines)
         q_copy(at, line, piece, at).wait_recv()
 
-        @pl.when(jnp.logical_not(last))
+        @pl.when((onward >= 0) & (onward < lines))
         def _():
             q_copy(at, onward, piece, at).start()
 
-        found = attend(at, piece)
-
-        @pl.when(last)
-        def _():
-            part_out[at, rows, :] = found.astype(jnp.bfloat16)
-            send_part(at, piece)
-
-        @pl.when(jnp.logical_not(last))
-        def _():
-            part_own[at, rows, :] = found
-
-    for distance in range(1, lines):
-
-        @pl.loop(0, pieces)
-        def _(piece):
-            @pl.when(line + distance < lines)
-            def _():
-                visit(line + distance, line - 1, piece)
-
-            @pl.when(line - distance >= 0)
-            def _():
-                visit(line - distance, line + 1, piece)
+        part_own[at, rows, :] = attend(at, piece, 0)
 
     @pl.loop(0, pieces)
     def _(piece):
@@ -526,29 +499,48 @@
             key = k_own[rows, lo : lo + DH].astype(jnp.float32)
             half = jnp.sum(query * key, axis=1, keepdims=True) * (0.5 * DH ** (-0.5))
             own.append(half_silu(half) * v_own[rows, lo : lo + DH].astype(jnp.float32))
-        total[rows, :] = attend(line, piece) + jnp.concatenate(own, axis=1)
-
-    def relay(turn):
-        inner = (2, 3, 0)[turn]
-        at = jnp.where(line == 1, inner, 3 - inner)
+        total[rows, :] = attend(line, piece, 0) + jnp.concatenate(own, axis=1)
+
+    for distance in range(1, lines):
+
+        @pl.loop(0, pieces)
+        def _(piece):
+            @pl.when(line + distance < lines)
+            def _():
+                visit(line + distance, line - 1, piece)
+
+            @pl.when(line - distance >= 0)
+            def _():
+                visit(line - distance, line + 1, piece)
+
+    part_copy(u_all, x_mp, u_sems, 1, across).wait_recv()
+    part_copy(u_all, x_mp, u_sems, 2, core).start()
+    keys_copy.wait_recv()
+    values_copy.wait_recv()
+
+    low = line < 2
+    for at in (jnp.where(low, 3, 0), jnp.where(low, 2, 1), jnp.where(low, 1 - line, 5 - line)):
+        gather(at, other_k, other_v, mate, 1)
 
         @pl.loop(0, pieces)
         def _(piece):
             rows = pl.ds(piece * SPAN, SPAN)
-            p_copy(at, line, at, piece).wait_recv()
-            part_out[at, rows, :] = (
-                part_own[at, rows, :] + part_in[at, rows, :].astype(jnp.float32)
-            ).astype(jnp.bfloat16)
+            part_own[at, rows, :] += attend(at, piece, 1)
+
+            @pl.when(above & below)
+            def _():
+                p_copy(at, line, at, piece).wait_recv()
+                part_own[at, rows, :] += part_in[at, rows, :].astype(jnp.float32)
+
+            part_out[at, rows, :] = part_own[at, rows, :].astype(jnp.bfloat16)
             send_part(at, piece)
 
-    @pl.when(above & below)
-    def _():
-        relay(0)
-        relay(1)
-        relay(2)
-
-    part_copy(u_all, x_mp, u_sems, 1, across).wait_recv()
-    part_copy(u_all, x_mp, u_sems, 2, core).start()
+    gather(line, other_k, other_v, mate, 1)
+
+    @pl.loop(0, pieces)
+    def _(piece):
+        total[pl.ds(piece * SPAN, SPAN), :] += attend(line, piece, 1)
+
 
     part_copy(u_all, core_mp, u_sems, 0, core).wait_recv()
     part_copy(u_all, far_mp, u_sems, 2, core).wait_recv()

time: 73.9 us -> 73.4 us (level)
  no operation moved by 1% of the time
where the time goes in v4:
time: 73.4 us; the launch traced here: 73.2 us
  Pallas kernels  70.8 us (96%)
  local copies, waits for them, and re-layouts  1.67 us (2%)
    pallas_call x1, Pallas kernels, move_queries(): pl.pallas_call(functools.partial(kernel, shards), out_shape=jax.ShapeDtyp...  70.8 us
    unnamed x1, local copies, waits for them, and re-layouts  1.67 us

profile of v4, /device:TPU:1, one launch (start us, length us, event | category | flops | bytes accessed | tf_op | source)
XLA Modules:
  0.0 73.2 jit_solution(14153510059386130428)
XLA Ops:
  0.7 70.8 %shard_map.100 = bf16[512,256]{1,0:T(8,128)(2,1)} custom-call(bf16[8,64,256]{2,1,0:T(8,128)(2,1)} %bitcast.1, s32[1,512]{1,0:T(1,128)} %perm.1, bf16[1024,4,256]{2,1,0:T(4,128)(2,1)} %w_in_far.1, bf16[256,1024]{1,0:T(8,128)(2,1)} %w_out.1, bf16[32,32,256]{2,1,0:T(8,128)(2,1)} %cache_k_far.1, bf16[32,32,256]{2,1,0:T(8,128)(2,1)} %cache_v_far.1, ...), custom_call_target="tpu_custom_call" | custom-call | flops 8000000000 | bytes 8388608 | tf_op jit(solution)/shard_map/pallas_call | solution.py:665
  71.5 1.7 %copy.13 = bf16[512,256]{1,0:T(8,128)(2,1)} copy(bf16[512,256]{1,0:T(8,128)(2,1)} %shard_map.100) | data formatting | bytes 524288

commit v5 on v4

--- a/solution.py
+++ b/solution.py
@@ -145,7 +145,7 @@
     shards,
     feats,
     perm,
-    w_in_far,
+    w_parts_far,
     w_out,
     cache_k_far,
     cache_v_far,
@@ -154,7 +154,6 @@
     home,
     slot,
     out,
-    w_in,
     cache_k,
     cache_v,
     w_parts,
@@ -226,7 +225,7 @@
         for index, (far, near) in enumerate(
             (
                 (feats.at[me], rows_all.at[mp, pl.ds(me * slots, slots)]),
-                (w_in_far, w_in),
+                (w_parts_far, w_parts),
                 (cache_k_far, cache_k),
                 (cache_v_far, cache_v),
                 (w_out.at[:, pl.ds(pl.multiple_of(mp * width, width), width)], wo_all.at[mp]),
@@ -313,14 +312,6 @@
     core_copy(me).start()
     x_copy(me).start()
 
-    loads[1].wait()
-
-    @pl.loop(0, w_in.shape[0], step=GROUP)
-    def _(first):
-        rows = pl.ds(pl.multiple_of(first, GROUP), GROUP)
-        for part in range(4):
-            w_parts[part, rows, :] = w_in[rows, part, :]
-
     for source in others:
         row_copy(source, me).wait_recv()
         core_copy(source).start()
@@ -339,6 +330,7 @@
             hist_v[at, begin : begin + BLK, :] = values_ref[place]
         hist_k[at, :, half * keys_here : (half + 1) * keys_here] = jnp.transpose(picked[...])
 
+    loads[1].wait()
     loads[2].wait()
     loads[3].wait()
     loads[4].wait()
@@ -668,7 +660,6 @@
         in_specs=[far, vmem] + [far] * 4 + [vmem] + [smem] * 3,
         out_specs=vmem,
         scratch_shapes=[
-            pltpu.VMEM(w_in.shape, bf16),
             pltpu.VMEM(cache_k.shape, bf16),
             pltpu.VMEM(cache_v.shape, bf16),
             pltpu.VMEM((4, full, width), bf16),
@@ -703,7 +694,7 @@
     )(
         cand_feats.reshape(shards, cands // shards, width),
         cand_perm,
-        w_in,
+        w_in.transpose(1, 0, 2),
         w_out,
         cache_k,
         cache_v,

time: 73.4 us -> 76.7 us (1.045)
  local copies, waits for them, and re-layouts: 1.67 us -> 4.89 us
    unnamed x1 -> x2, local copies, waits for them, and re-layouts: 1.67 us -> 4.89 us
where the time goes in v5:
time: 76.7 us; the launch traced here: 76.5 us
  Pallas kernels  70.9 us (92%)
  local copies, waits for them, and re-layouts  4.89 us (6%)
    pallas_call x1, Pallas kernels, move_queries(): pl.pallas_call(functools.partial(kernel, shards), out_shape=jax.ShapeDtyp...  70.9 us
    unnamed x2, local copies, waits for them, and re-layouts  4.89 us

profile of v5, /device:TPU:1, one launch (start us, length us, event | category | flops | bytes accessed | tf_op | source)
XLA Modules:
  0.0 76.5 jit_solution(5261299424899068381)
XLA Ops:
  0.7 3.2 %copy.13 = bf16[1024,4,256]{2,0,1:T(8,128)(2,1)} copy(bf16[1024,4,256]{2,1,0:T(4,128)(2,1)} %param.12) | data formatting | bytes 4194304 | tf_op args[2]
  3.9 70.9 %shard_map.100 = bf16[512,256]{1,0:T(8,128)(2,1)} custom-call(bf16[8,64,256]{2,1,0:T(8,128)(2,1)} %bitcast.5, s32[1,512]{1,0:T(1,128)} %perm.1, bf16[4,1024,256]{2,1,0:T(8,128)(2,1)} %bitcast.4, bf16[256,1024]{1,0:T(8,128)(2,1)} %w_out.1, bf16[32,32,256]{2,1,0:T(8,128)(2,1)} %cache_k_far.1, bf16[32,32,256]{2,1,0:T(8,128)(2,1)} %cache_v_far.1, ...), custom_call_target="tpu_custom_call" | custom-call | flops 8000000000 | bytes 8388608 | tf_op jit(solution)/shard_map/pallas_call | solution.py:657
  74.8 1.7 %copy.16 = bf16[512,256]{1,0:T(8,128)(2,1)} copy(bf16[512,256]{1,0:T(8,128)(2,1)} %shard_map.100) | data formatting | bytes 524288

commit v6 on v4

--- a/solution.py
+++ b/solution.py
@@ -295,8 +295,12 @@
             chunk(far_mp, source), chunk(far_mp, source), fwd_s.at[source], fwd_r.at[source], core
         )
 
-    keys_copy = remote(cache_k_far, other_k, kv_s.at[0], kv_r.at[0], side_mate)
-    values_copy = remote(cache_v_far, other_v, kv_s.at[1], kv_r.at[1], side_mate)
+    share = cache_k.shape[0] // 8
+
+    def cache_copy(index):
+        near, other = ((cache_k_far, other_k), (cache_v_far, other_v))[index // 8]
+        blocks = pl.ds(index % 8 * share, share)
+        return remote(near.at[blocks], other.at[blocks], kv_s.at[index], kv_r.at[index], side_mate)
 
     for target in others[::-1]:
         row_copy(me, target).start()
@@ -306,8 +310,8 @@
     counts[0:groups, :] = (block_mask[0] * jnp.clip(length[0] - places, 0, BLK)).astype(jnp.float32)
     for step in range(1, lines):
         count_copy(line, (line + step) % lines).start()
-    keys_copy.start()
-    values_copy.start()
+    for index in range(4):
+        cache_copy(index).start()
     loads[0].wait()
     counts_all[line] = counts[...]
     core_copy(me).start()
@@ -321,10 +325,11 @@
         for part in range(4):
             w_parts[part, rows, :] = w_in[rows, part, :]
 
-    for source in others:
+    for index, source in enumerate(others, 4):
         row_copy(source, me).wait_recv()
         core_copy(source).start()
         x_copy(source).start()
+        cache_copy(index).start()
 
     for step in range(1, 4):
         out_weight_copy(mp, (mp + step) % 4).start()
@@ -347,9 +352,11 @@
     def _(at):
         gather(at, cache_k, cache_v, me, 0)
 
-    for source in [me] + others:
+    for index, source in enumerate([me] + others, 11):
         x_got(source).wait_recv()
         fwd_copy(source).start()
+        if index < 16:
+            cache_copy(index).start()
 
     for step in range(1, lines):
         count_copy((line + step) % lines, line).wait_recv()
@@ -515,8 +522,8 @@
 
     part_copy(u_all, x_mp, u_sems, 1, across).wait_recv()
     part_copy(u_all, x_mp, u_sems, 2, core).start()
-    keys_copy.wait_recv()
-    values_copy.wait_recv()
+    for index in range(16):
+        cache_copy(index).wait_recv()
 
     low = line < 2
     for at in (jnp.where(low, 3, 0), jnp.where(low, 2, 1), jnp.where(low, 1 - line, 5 - line)):
@@ -614,8 +621,8 @@
         x_copy(source).wait_send()
         fwd_copy(source).wait_send()
 
-    keys_copy.wait_send()
-    values_copy.wait_send()
+    for index in range(16):
+        cache_copy(index).wait_send()
     for step in range(1, lines):
         count_copy(line, (line + step) % lines).wait_send()
     for step in range(1, 4):
@@ -661,7 +668,7 @@
     smem = pl.BlockSpec(memory_space=pltpu.SMEM)
     far = pl.BlockSpec(memory_space=pl.ANY)
     lots = (lines + 1) * pieces
-    pairs = [shards, shards, shards, shards, 2, lines, 4, lots, lots, 3, 3 * pieces]
+    pairs = [shards, shards, shards, shards, 16, lines, 4, lots, lots, 3, 3 * pieces]
     return pl.pallas_call(
         functools.partial(kernel, shards),
         out_shape=jax.ShapeDtypeStruct((cands, width), bf16),

time: 73.4 us -> 73.6 us (level)
  no operation moved by 1% of the time
where the time goes in v6:
time: 73.6 us; the launch traced here: 73.5 us
  Pallas kernels  71.1 us (97%)
  local copies, waits for them, and re-layouts  1.67 us (2%)
    pallas_call x1, Pallas kernels, move_queries(): pl.pallas_call(functools.partial(kernel, shards), out_shape=jax.ShapeDtyp...  71.1 us
    unnamed x1, local copies, waits for them, and re-layouts  1.67 us

profile of v6, /device:TPU:1, one launch (start us, length us, event | category | flops | bytes accessed | tf_op | source)
XLA Modules:
  0.0 73.5 jit_solution(9962618627612233119)
XLA Ops:
  0.7 71.1 %shard_map.100 = bf16[512,256]{1,0:T(8,128)(2,1)} custom-call(bf16[8,64,256]{2,1,0:T(8,128)(2,1)} %bitcast.1, s32[1,512]{1,0:T(1,128)} %perm.1, bf16[1024,4,256]{2,1,0:T(4,128)(2,1)} %w_in_far.1, bf16[256,1024]{1,0:T(8,128)(2,1)} %w_out.1, bf16[32,32,256]{2,1,0:T(8,128)(2,1)} %cache_k_far.1, bf16[32,32,256]{2,1,0:T(8,128)(2,1)} %cache_v_far.1, ...), custom_call_target="tpu_custom_call" | custom-call | flops 8000000000 | bytes 8388608 | tf_op jit(solution)/shard_map/pallas_call | solution.py:672
  71.8 1.7 %copy.13 = bf16[512,256]{1,0:T(8,128)(2,1)} copy(bf16[512,256]{1,0:T(8,128)(2,1)} %shard_map.100) | data formatting | bytes 524288

commit v7 on v4

--- a/solution.py
+++ b/solution.py
@@ -137,7 +137,7 @@
     return half + half * jnp.tanh(half)
 
 
-SPAN = 256
+SPAN = 128
 TILE = 256
 
 
@@ -501,8 +501,9 @@
             own.append(half_silu(half) * v_own[rows, lo : lo + DH].astype(jnp.float32))
         total[rows, :] = attend(line, piece, 0) + jnp.concatenate(own, axis=1)
 
-    for distance in range(1, lines):
-
+    mid = above & below
+
+    def meet(distance):
         @pl.loop(0, pieces)
         def _(piece):
             @pl.when(line + distance < lines)
@@ -513,34 +514,49 @@
             def _():
                 visit(line - distance, line + 1, piece)
 
+    def complete(at):
+        gather(at, other_k, other_v, mate, 1)
+
+        @pl.loop(0, pieces)
+        def _(piece):
+            rows = pl.ds(piece * SPAN, SPAN)
+            part_own[at, rows, :] += attend(at, piece, 1)
+
+            @pl.when(mid)
+            def _():
+                p_copy(at, line, at, piece).wait_recv()
+                part_own[at, rows, :] += part_in[at, rows, :].astype(jnp.float32)
+
+            part_out[at, rows, :] = part_own[at, rows, :].astype(jnp.bfloat16)
+            send_part(at, piece)
+
+    def complete_own():
+        gather(line, other_k, other_v, mate, 1)
+
+        @pl.loop(0, pieces)
+        def _(piece):
+            total[pl.ds(piece * SPAN, SPAN), :] += attend(line, piece, 1)
+
+    meet(1)
+    meet(2)
     part_copy(u_all, x_mp, u_sems, 1, across).wait_recv()
     part_copy(u_all, x_mp, u_sems, 2, core).start()
     keys_copy.wait_recv()
     values_copy.wait_recv()
-
     low = line < 2
-    for at in (jnp.where(low, 3, 0), jnp.where(low, 2, 1), jnp.where(low, 1 - line, 5 - line)):
-        gather(at, other_k, other_v, mate, 1)
-
-        @pl.loop(0, pieces)
-        def _(piece):
-            rows = pl.ds(piece * SPAN, SPAN)
-            part_own[at, rows, :] += attend(at, piece, 1)
-
-            @pl.when(above & below)
-            def _():
-                p_copy(at, line, at, piece).wait_recv()
-                part_own[at, rows, :] += part_in[at, rows, :].astype(jnp.float32)
-
-            part_out[at, rows, :] = part_own[at, rows, :].astype(jnp.bfloat16)
-            send_part(at, piece)
-
-    gather(line, other_k, other_v, mate, 1)
-
-    @pl.loop(0, pieces)
-    def _(piece):
-        total[pl.ds(piece * SPAN, SPAN), :] += attend(line, piece, 1)
-
+
+    @pl.when(mid)
+    def _():
+        complete_own()
+
+    complete(jnp.where(low, line + 1, line - 1))
+    complete(jnp.where(low, line + 2, line - 2))
+    meet(3)
+    complete(jnp.where(mid, 3 * (line - 1), 3 - line))
+
+    @pl.when(jnp.logical_not(mid))
+    def _():
+        complete_own()
 
     part_copy(u_all, core_mp, u_sems, 0, core).wait_recv()
     part_copy(u_all, far_mp, u_sems, 2, core).wait_recv()

time: 73.4 us -> 75.9 us (1.034)
  Pallas kernels: 70.8 us -> 73.4 us
    pallas_call x1, Pallas kernels: 70.8 us -> 73.4 us  [move_queries(): pl.pallas_call(functools.partial(kernel, shards), out_shape=jax.ShapeDtyp...]
where the time goes in v7:
time: 75.9 us; the launch traced here: 75.7 us
  Pallas kernels  73.4 us (97%)
  local copies, waits for them, and re-layouts  1.67 us (2%)
    pallas_call x1, Pallas kernels, move_queries(): pl.pallas_call(functools.partial(kernel, shards), out_shape=jax.ShapeDtyp...  73.4 us
    unnamed x1, local copies, waits for them, and re-layouts  1.67 us

profile of v7, /device:TPU:1, one launch (start us, length us, event | category | flops | bytes accessed | tf_op | source)
XLA Modules:
  0.0 75.7 jit_solution(14212981040851945784)
XLA Ops:
  0.7 73.4 %shard_map.100 = bf16[512,256]{1,0:T(8,128)(2,1)} custom-call(bf16[8,64,256]{2,1,0:T(8,128)(2,1)} %bitcast.1, s32[1,512]{1,0:T(1,128)} %perm.1, bf16[1024,4,256]{2,1,0:T(4,128)(2,1)} %w_in_far.1, bf16[256,1024]{1,0:T(8,128)(2,1)} %w_out.1, bf16[32,32,256]{2,1,0:T(8,128)(2,1)} %cache_k_far.1, bf16[32,32,256]{2,1,0:T(8,128)(2,1)} %cache_v_far.1, ...), custom_call_target="tpu_custom_call" | custom-call | flops 8000000000 | bytes 8388608 | tf_op jit(solution)/shard_map/pallas_call | solution.py:681
  74.0 1.7 %copy.13 = bf16[512,256]{1,0:T(8,128)(2,1)} copy(bf16[512,256]{1,0:T(8,128)(2,1)} %shard_map.100) | data formatting | bytes 524288

commit v8 on v7

--- a/solution.py
+++ b/solution.py
@@ -137,7 +137,7 @@
     return half + half * jnp.tanh(half)
 
 
-SPAN = 128
+SPAN = 256
 TILE = 256
 
 
@@ -675,7 +675,7 @@
     bf16, f32 = jnp.bfloat16, jnp.float32
     vmem = pl.BlockSpec(memory_space=pltpu.VMEM)
     smem = pl.BlockSpec(memory_space=pltpu.SMEM)
-    far = pl.BlockSpec(memory_space=pl.ANY)
+    far = pl.BlockSpec(memory_space=pltpu.HBM)
     lots = (lines + 1) * pieces
     pairs = [shards, shards, shards, shards, 2, lines, 4, lots, lots, 3, 3 * pieces]
     return pl.pallas_call(
@@ -713,7 +713,7 @@
         + [pltpu.SemaphoreType.DMA((count,)) for count in pairs for _ in range(2)]
         + [pltpu.SemaphoreType.DMA((5,))],
         compiler_params=pltpu.CompilerParams(
-            collective_id=0, has_side_effects=True, vmem_limit_bytes=56 * 1024 * 1024
+            collective_id=0, has_side_effects=True, vmem_limit_bytes=40 * 1024 * 1024
         ),
         cost_estimate=pl.CostEstimate(flops=8 * 10**9, bytes_accessed=2**23, transcendentals=2**22),
     )(

time: 75.9 us -> 80.5 us (1.061); the launches traced: 75.7 us -> 79.5 us
  local copies, waits for them, and re-layouts: 1.67 us -> 9.07 us
  Pallas kernels: 73.4 us -> 69.8 us
    unnamed x1 -> x19, local copies, waits for them, and re-layouts: 1.67 us -> 9.07 us
    pallas_call x1, Pallas kernels: 73.4 us -> 69.8 us  [move_queries(): pl.pallas_call(functools.partial(kernel, shards), out_shape=jax.ShapeDtyp...]
where the time goes in v8:
time: 80.5 us; the launch traced here: 79.5 us
  Pallas kernels  69.8 us (87%)
  local copies, waits for them, and re-layouts  9.07 us (11%)
    pallas_call x1, Pallas kernels, move_queries(): pl.pallas_call(functools.partial(kernel, shards), out_shape=jax.ShapeDtyp...  69.8 us
    unnamed x19, local copies, waits for them, and re-layouts  9.07 us

profile of v8, /device:TPU:1, one launch (start us, length us, event | category | flops | bytes accessed | tf_op | source)
XLA Modules:
  0.0 79.5 jit_solution(3559868397695584186)
XLA Ops:
  0.7 0.0 copy-start
  0.7 1.6 %copy-done = bf16[1024,4,256]{2,1,0:T(4,128)(2,1)S(1)} copy-done((bf16[1024,4,256]{2,1,0:T(4,128)(2,1)S(1)}, bf16[1024,4,256]{2,1,0:T(4,128)(2,1)}, u32[]{:S(2)}) %copy-start) | copy-done | bytes 2097176
  2.2 0.0 copy-start.1
  2.2 1.0 %copy-done.1 = bf16[256,1024]{1,0:T(8,128)(2,1)S(1)} copy-done((bf16[256,1024]{1,0:T(8,128)(2,1)S(1)}, bf16[256,1024]{1,0:T(8,128)(2,1)}, u32[]{:S(2)}) %copy-start.1) | copy-done | bytes 524312
  3.3 0.0 copy-start.2
  3.3 1.0 %copy-done.2 = bf16[32,32,256]{2,1,0:T(8,128)(2,1)S(1)} copy-done((bf16[32,32,256]{2,1,0:T(8,128)(2,1)S(1)}, bf16[32,32,256]{2,1,0:T(8,128)(2,1)}, u32[]{:S(2)}) %copy-start.2) | copy-done | bytes 524312
  4.3 0.0 copy-start.3
  4.3 1.0 %copy-done.3 = bf16[32,32,256]{2,1,0:T(8,128)(2,1)S(1)} copy-done((bf16[32,32,256]{2,1,0:T(8,128)(2,1)S(1)}, bf16[32,32,256]{2,1,0:T(8,128)(2,1)}, u32[]{:S(2)}) %copy-start.3) | copy-done | bytes 524312
  5.4 0.0 copy-start.4
  5.4 0.9 %copy-done.4 = bf16[512,256]{1,0:T(8,128)(2,1)S(1)} copy-done((bf16[512,256]{1,0:T(8,128)(2,1)S(1)}, bf16[512,256]{1,0:T(8,128)(2,1)}, u32[]{:S(2)}) %copy-start.4) | copy-done | bytes 262168
  6.3 0.0 copy-start.5
  6.3 0.7 copy-done.5
  7.0 0.0 copy-start.6
  7.0 0.7 copy-done.6
  7.7 0.0 copy-start.7
  7.7 0.7 copy-done.7
  8.4 0.0 copy-start.8
  8.4 0.7 copy-done.8
  9.0 69.8 %shard_map.100 = bf16[512,256]{1,0:T(8,128)(2,1)S(1)} custom-call(bf16[8,64,256]{2,1,0:T(8,128)(2,1)S(1)} %bitcast.1, s32[1,512]{1,0:T(1,128)S(1)} %copy-done.6, bf16[1024,4,256]{2,1,0:T(4,128)(2,1)S(1)} %copy-done, bf16[256,1024]{1,0:T(8,128)(2,1)S(1)} %copy-done.1, bf16[32,32,256]{2,1,0:T(8,128)(2,1)S(1)} %copy-done.2, bf16[32,32,256]{2,1,0:T(8,128)(2,1)S(1)} %copy-done.3, ...), custom_call_target="tpu_custom_call" | custom-call | flops 8000000000 | bytes 8388608 | tf_op jit(solution)/shard_map/pallas_call | solution.py:681
  78.8 0.7 copy.13
Async XLA Ops:
  0.7 1.6 %copy-start = (bf16[1024,4,256]{2,1,0:T(4,128)(2,1)S(1)}, bf16[1024,4,256]{2,1,0:T(4,128)(2,1)}, u32[]{:S(2)}) copy-start(bf16[1024,4,256]{2,1,0:T(4,128)(2,1)} %w_in_far.1) | copy-start | bytes 6291460
  2.2 1.0 %copy-start.1 = (bf16[256,1024]{1,0:T(8,128)(2,1)S(1)}, bf16[256,1024]{1,0:T(8,128)(2,1)}, u32[]{:S(2)}) copy-start(bf16[256,1024]{1,0:T(8,128)(2,1)} %w_out.1) | copy-start | bytes 1572868
  3.3 1.0 %copy-start.2 = (bf16[32,32,256]{2,1,0:T(8,128)(2,1)S(1)}, bf16[32,32,256]{2,1,0:T(8,128)(2,1)}, u32[]{:S(2)}) copy-start(bf16[32,32,256]{2,1,0:T(8,128)(2,1)} %cache_k_far.1) | copy-start | bytes 1572868
  4.3 1.0 %copy-start.3 = (bf16[32,32,256]{2,1,0:T(8,128)(2,1)S(1)}, bf16[32,32,256]{2,1,0:T(8,128)(2,1)}, u32[]{:S(2)}) copy-start(bf16[32,32,256]{2,1,0:T(8,128)(2,1)} %cache_v_far.1) | copy-start | bytes 1572868
  5.4 0.9 %copy-start.4 = (bf16[512,256]{1,0:T(8,128)(2,1)S(1)}, bf16[512,256]{1,0:T(8,128)(2,1)}, u32[]{:S(2)}) copy-start(bf16[512,256]{1,0:T(8,128)(2,1)} %param.10) | copy-start | bytes 786436
  6.3 0.7 copy-start.5
  7.0 0.7 copy-start.6
  7.7 0.7 copy-start.7
  8.4 0.7 copy-start.8
